TPU v7x, 256 devices: a whole 4x4x8 slice. The times are simulated.
256 devices in a mesh: blk: 8 (over y, x_hi), dp: 32 (over x_lo, z, core).
Axes of the slice: x: 4 (x_hi: 2, x_lo: 2; x = x_hi * 2 + x_lo), y: 4, z: 8, core: 2. Of those that a mesh axis runs over, the one named last changes fastest.
Arguments:
- patches: bfloat16 [32768, 64, 256], P(('blk', 'dp')), may hold values from -6 to 6
- w_mix: bfloat16 [256, 128], replicated, may hold values from -0.375 to 0.375
- w_in: bfloat16 [2048, 512], replicated, may hold values from -0.125 to 0.125
- w_out: bfloat16 [512, 128], replicated, may hold values from -0.25 to 0.25
- partner_dev: int32 [32768], P(('blk', 'dp')), may hold values from 0 to 31, as said below
- partner_row: int32 [32768], P(('blk', 'dp')), may hold values from 0 to 127, as said below
Outputs:
- loss_rows: float32 [32768], P(('blk', 'dp'))
- grad_mix: float32 [256, 128], replicated
- grad_in: float32 [2048, 512], replicated
- grad_out: float32 [512, 128], replicated
Inputs may be any that keep to these rules, and one draw needn't show every extreme that they name: Among one device's rows every dp index appears as partner_dev exactly 128/32 times. Over the rows that share a blk index, the pairs (partner_dev, partner_row) name every pair of dp index and row of a device exactly once.
All inputs are finite; a program needn't handle non-finite values.
Results may differ from a plain program's by a relative error of at most 0.012.
The roundings to bfloat16 on the way count: a program that leaves them out, or rounds other values in their place, can miss the bound.
Values may be sent and summed in bfloat16 or wider, within the bound.
A program may use at most 64 MiB of HBM per device.

v0:
```python
import math

import jax
import jax.numpy as jnp
from jax import lax
from jax.sharding import PartitionSpec as P

SCALE = 10.0


def dft_table(length, freqs):
    angle_idx = jnp.arange(length, dtype=jnp.int32)
    freq_idx = jnp.arange(freqs, dtype=jnp.int32)
    phase = jnp.mod(freq_idx[None, :] * angle_idx[:, None], length).astype(jnp.float32) * (
        2.0 * math.pi / length
    )
    return jnp.concatenate([jnp.cos(phase), -jnp.sin(phase)], axis=1).astype(jnp.bfloat16)


def encode(block, w_mix, w_in, w_out):
    count, length, lanes = block.shape
    filters = w_mix.shape[1]
    freqs = w_in.shape[0] // filters
    angle_table = dft_table(length, freqs)
    spec = jnp.einsum("pac,ak->pkc", block, angle_table, preferred_element_type=jnp.float32).astype(
        jnp.bfloat16
    )
    mixed = jnp.dot(spec.reshape(-1, lanes), w_mix, preferred_element_type=jnp.float32).reshape(
        count, 2 * freqs, filters
    )
    real_part = mixed[:, :freqs]
    imag_part = mixed[:, freqs:]
    powers = real_part * real_part + imag_part * imag_part
    features = jnp.log1p(powers).reshape(count, -1)
    mean_removed = features - jnp.mean(features, axis=1, keepdims=True)
    reciprocal_scale = lax.rsqrt(
        jnp.mean(mean_removed * mean_removed, axis=1, keepdims=True) + 1e-05
    )
    normed = (mean_removed * reciprocal_scale).astype(jnp.bfloat16)
    preact = jnp.dot(normed, w_in, preferred_element_type=jnp.float32)
    hidden = jax.nn.silu(preact).astype(jnp.bfloat16)
    raw_embed = jnp.dot(hidden, w_out, preferred_element_type=jnp.float32)
    norms = jnp.sqrt(jnp.sum(raw_embed * raw_embed, axis=1, keepdims=True) + 1e-06)
    unit32 = raw_embed / norms
    saved = (
        spec,
        real_part,
        imag_part,
        powers,
        mean_removed,
        reciprocal_scale,
        normed,
        preact,
        hidden,
        unit32,
        norms,
    )
    return (unit32.astype(jnp.bfloat16), saved)


def back_upper(grad_units, saved, w_in, w_out):
    (
        spec,
        real_part,
        imag_part,
        powers,
        mean_removed,
        reciprocal_scale,
        normed,
        preact,
        hidden,
        unit32,
        norms,
    ) = saved
    grad_raw = (
        (grad_units - unit32 * jnp.sum(unit32 * grad_units, axis=1, keepdims=True)) / norms
    ).astype(jnp.bfloat16)
    g_out = jnp.dot(hidden.T, grad_raw, preferred_element_type=jnp.float32)
    grad_hid = jnp.dot(grad_raw, w_out.T, preferred_element_type=jnp.float32)
    sigm = jax.nn.sigmoid(preact)
    grad_pre = (grad_hid * sigm * (1.0 + preact * (1.0 - sigm))).astype(jnp.bfloat16)
    g_in = jnp.dot(normed.T, grad_pre, preferred_element_type=jnp.float32)
    norm_gradient = jnp.dot(grad_pre, w_in.T, preferred_element_type=jnp.float32)
    return (g_in, g_out, norm_gradient)


def back_lower(norm_gradient, saved):
    (
        spec,
        real_part,
        imag_part,
        powers,
        mean_removed,
        reciprocal_scale,
        normed,
        preact,
        hidden,
        unit32,
        norms,
    ) = saved
    lanes = spec.shape[2]
    normalized_input = mean_removed * reciprocal_scale
    feature_gradient = reciprocal_scale * (
        norm_gradient
        - jnp.mean(norm_gradient, axis=1, keepdims=True)
        - normalized_input * jnp.mean(norm_gradient * normalized_input, axis=1, keepdims=True)
    )
    grad_pow = feature_gradient.reshape(powers.shape) / (1.0 + powers)
    grad_mixed = jnp.concatenate(
        [2.0 * real_part * grad_pow, 2.0 * imag_part * grad_pow], axis=1
    ).astype(jnp.bfloat16)
    return jnp.dot(
        spec.reshape(-1, lanes).T,
        grad_mixed.reshape(-1, grad_mixed.shape[2]),
        preferred_element_type=jnp.float32,
    )


def negative_part(units, piece, row_ids):
    scores = SCALE * jnp.dot(units, piece.T, preferred_element_type=jnp.float32)
    column = jnp.arange(piece.shape[0], dtype=jnp.int32)
    expo = jnp.where(column[None, :] == row_ids[:, None], jnp.float32(0.0), jnp.exp(scores))
    return (
        jnp.sum(expo, axis=1),
        jnp.dot(expo.astype(jnp.bfloat16), piece, preferred_element_type=jnp.float32),
    )


def key_part(units, piece, tot_piece, row_ids):
    scores = SCALE * jnp.dot(piece, units.T, preferred_element_type=jnp.float32)
    column = jnp.arange(piece.shape[0], dtype=jnp.int32)
    expo = jnp.where(column[:, None] == row_ids[None, :], jnp.float32(0.0), jnp.exp(scores))
    weights = (expo / tot_piece[:, None]).astype(jnp.bfloat16)
    return jnp.dot(weights.T, piece, preferred_element_type=jnp.float32)


def on_device(patches, w_mix, w_in, w_out, partner_dev, partner_row):
    count = patches.shape[0]
    embed = w_out.shape[1]
    units, saved = encode(patches, w_mix, w_in, w_out)
    peers = lax.axis_size("dp")
    per_peer = count // peers
    sorted_positions = jnp.argsort(partner_dev, stable=True)
    inverse = jnp.argsort(sorted_positions, stable=True)
    wanted = partner_row[sorted_positions].reshape(peers, per_peer)
    asked = lax.all_to_all(wanted, "dp", split_axis=0, concat_axis=0, tiled=True)
    picked = units[asked]
    returned_rows = lax.all_to_all(picked, "dp", split_axis=0, concat_axis=0, tiled=True)
    positive = returned_rows.reshape(count, embed)[inverse]
    spos = SCALE * jnp.sum(units.astype(jnp.float32) * positive.astype(jnp.float32), axis=1)
    row_ids = lax.axis_index("blk") * count + jnp.arange(count, dtype=jnp.int32)
    zpart, npart = negative_part(units, lax.all_gather(units, "blk", axis=0, tiled=True), row_ids)
    totals = jnp.exp(spos) + zpart
    all_totals = lax.all_gather(totals, "blk", axis=0, tiled=True)
    keyterm = key_part(units, lax.all_gather(units, "blk", axis=0, tiled=True), all_totals, row_ids)
    loss_rows = jnp.log(totals) - spos
    coef = SCALE / count
    ppos = jnp.exp(spos) / totals
    partner_grad = coef * (ppos - 1.0)[:, None] * units.astype(jnp.float32)
    outgoing = partner_grad[sorted_positions].reshape(peers, per_peer, embed)
    incoming = lax.all_to_all(outgoing, "dp", split_axis=0, concat_axis=0, tiled=True)
    from_partner = (
        jnp.zeros((count, embed), jnp.float32)
        .at[asked.reshape(-1)]
        .add(incoming.reshape(-1, embed))
    )
    grad_units = (
        coef * ((ppos - 1.0)[:, None] * positive.astype(jnp.float32) + npart / totals[:, None])
        + coef * keyterm
        + from_partner
    )
    g_in, g_out, norm_gradient = back_upper(grad_units, saved, w_in, w_out)
    g_mix = back_lower(norm_gradient, saved)
    g_mix, g_in, g_out = lax.psum((g_mix, g_in, g_out), ("blk", "dp"))
    return (loss_rows, g_mix, g_in, g_out)


def solution(mesh):
    placed = (P(("blk", "dp"), None, None), P(), P(), P(), P(("blk", "dp")), P(("blk", "dp")))
    return jax.shard_map(
        on_device,
        mesh=mesh,
        in_specs=placed,
        out_specs=(P(("blk", "dp")), P(), P(), P()),
        check_vma=False,
    )
```

profile of v0, /device:TPU:1, one launch (start us, length us, event | category | flops | bytes accessed | tf_op | source)
XLA Modules:
  0.0 422.5 jit_solution(2403587534280122232)
XLA Ops:
  7.2 3.3 sort.31
  10.5 1.6 gather_fusion
  12.8 11.0 %all-to-all-start = ((s32[32,1,4]{2,1,0:T(1,128)}), s32[32,1,4]{2,1,0:T(1,128)S(1)}, u32[]{:S(2)}, u32[]{:S(2)}) async-start(s32[32,1,4]{2,1,0:T(1,128)} %bitcast.4), calls=%async_computation | async-start | bytes 32768 | tf_op jit(solution)/shard_map/all_to_all | solution.py:146
  24.0 2.5 sort.32
  26.5 2.9 convert_bitcast_fusion
  29.5 2.5 fusion
  33.7 1.6 copy.42
  36.8 26.6 %all_gather.7 = bf16[1024,128]{0,1:T(8,128)(2,1)S(1)} all-gather(bf16[128,128]{0,1:T(8,128)(2,1)S(1)} %fusion.35), channel_id=1, replica_groups=mesh['blk'=8,'dp'=32] {'blk'}, dimensions={0}, use_global_device_ids=true | all-gather | bytes 294912 | tf_op jit(solution)/shard_map/all_gather | solution.py:152
  67.5 13.3 %all-to-all-start.1 = ((bf16[32,4,128]{2,1,0:T(4,128)(2,1)}), bf16[32,4,128]{2,1,0:T(4,128)(2,1)S(1)}, u32[]{:S(2)}, u32[]{:S(2)}) async-start(bf16[32,4,128]{2,1,0:T(4,128)(2,1)} %bitcast.6), calls=%async_computation.1 | async-start | bytes 65536 | tf_op jit(solution)/shard_map/all_to_all | solution.py:148
  81.4 7.3 %all-to-all-done.1 = bf16[32,4,128]{2,1,0:T(4,128)(2,1)S(1)} async-done(((bf16[32,4,128]{2,1,0:T(4,128)(2,1)}), bf16[32,4,128]{2,1,0:T(4,128)(2,1)S(1)}, u32[]{:S(2)}, u32[]{:S(2)}) %all-to-all-start.1) | async-done | bytes 32800 | tf_op jit(solution)/shard_map/all_to_all | solution.py:148
  90.2 18.6 %all-gather = f32[8,1,128]{2,1,0:T(1,128)} all-gather(f32[1,1,128]{2,1,0:T(1,128)S(1)} %bitcast.48), channel_id=1, replica_groups=mesh['blk'=8,'dp'=32] {'blk'}, dimensions={0}, use_global_device_ids=true | all-gather | bytes 4608 | tf_op jit(solution)/shard_map/all_gather | solution.py:154
  110.1 8.3 %all-to-all-start.2 = ((f32[32,4,128]{2,1,0:T(4,128)}), f32[32,4,128]{2,1,0:T(4,128)S(1)}, u32[]{:S(2)}, u32[]{:S(2)}) async-start(f32[32,4,128]{2,1,0:T(4,128)} %bitcast.11), calls=%async_computation.2 | async-start | bytes 131072 | tf_op jit(solution)/shard_map/all_to_all | solution.py:161
  119.8 2.2 fusion.12
  122.8 3.8 all-to-all-done.2
  126.6 1.5 scatter_fusion
  128.2 1.8 fusion.44
  132.2 2.8 fusion.36
  136.4 1.5 copy.54
  138.0 2.0 multiply_convert_fusion.1
  140.1 1.7 copy.55
  141.8 3.3 convolution_bitcast_fusion
  146.2 262.5 %all-reduce.3.cloned.1.call-done = (f32[256,128]{1,0:T(8,128)}, f32[2048,512]{1,0:T(8,128)}, f32[512,128]{1,0:T(8,128)}) async-done(((f32[256,128]{1,0:T(8,128)}, f32[2048,512]{1,0:T(8,128)}, f32[512,128]{1,0:T(8,128)}), (f32[256,128]{1,0:T(8,128)}, f32[2048,512]{1,0:T(8,128)}, f32[512,128]{1,0:T(8,128)})) %all-reduce.3.cloned.1.call-update) | async-done | bytes 4587536 | tf_op jit(solution)/shard_map/psum | solution.py:174
  408.7 1.6 copy.66
  410.3 4.7 %copy.67 = f32[2048,512]{1,0:T(8,128)} copy(f32[2048,512]{1,0:T(8,128)} %get-tuple-element.33) | data formatting | bytes 8388608
  (81 shorter events, 19.1 us)
Async XLA Ops:
  7.2 28.1 %copy-start = (bf16[2048,512]{1,0:T(8,128)(2,1)S(1)}, bf16[2048,512]{1,0:T(8,128)(2,1)}, u32[]{:S(2)}) copy-start(bf16[2048,512]{1,0:T(8,128)(2,1)} %param.8) | copy-start | bytes 6291460
  12.8 51.7 %all-to-all-start = ((s32[32,1,4]{2,1,0:T(1,128)}), s32[32,1,4]{2,1,0:T(1,128)S(1)}, u32[]{:S(2)}, u32[]{:S(2)}) async-start(s32[32,1,4]{2,1,0:T(1,128)} %bitcast.4), calls=%async_computation | async-start | bytes 32768 | tf_op jit(solution)/shard_map/all_to_all | solution.py:146
  24.0 39.4 %copy-start.14 = (s32[128]{0:T(128)}, s32[128]{0:T(128)S(1)}, u32[]{:S(2)}) copy-start(s32[128]{0:T(128)S(1)} %iota_add_fusion) | copy-start | bytes 1540
  26.5 2.9 copy-start.8
  29.5 2.5 copy-start.3
  32.0 1.3 copy-start.1
  32.5 1.2 copy-start.2
  35.3 1.2 copy-start.6
  36.5 27.9 %copy-start.7 = (bf16[128,512]{1,0:T(8,128)(2,1)}, bf16[128,512]{1,0:T(8,128)(2,1)S(1)}, u32[]{:S(2)}) copy-start(bf16[128,512]{1,0:T(8,128)(2,1)S(1)} %get-tuple-element.20) | copy-start | bytes 393220
  63.4 1.0 copy-start.4
  67.5 21.3 %all-to-all-start.1 = ((bf16[32,4,128]{2,1,0:T(4,128)(2,1)}), bf16[32,4,128]{2,1,0:T(4,128)(2,1)S(1)}, u32[]{:S(2)}, u32[]{:S(2)}) async-start(bf16[32,4,128]{2,1,0:T(4,128)(2,1)} %bitcast.6), calls=%async_computation.1 | async-start | bytes 65536 | tf_op jit(solution)/shard_map/all_to_all | solution.py:148
  89.6 19.2 %copy-start.9 = (f32[128]{0:T(128)}, f32[128]{0:T(128)S(1)}, u32[]{:S(2)}) copy-start(f32[128]{0:T(128)S(1)} %fusion.21) | copy-start | bytes 1540
  90.2 18.6 %copy-start.11 = (f32[128]{0:T(128)}, f32[128]{0:T(128)S(1)}, u32[]{:S(2)}) copy-start(f32[128]{0:T(128)S(1)} %get-tuple-element.15) | copy-start | bytes 1540
  110.1 16.5 %copy-start.13 = (s32[128]{0:T(128)S(1)}, s32[128]{0:T(128)}, u32[]{:S(2)}) copy-start(s32[128]{0:T(128)} %fusion.31) | copy-start | bytes 1540
  110.1 16.5 %all-to-all-start.2 = ((f32[32,4,128]{2,1,0:T(4,128)}), f32[32,4,128]{2,1,0:T(4,128)S(1)}, u32[]{:S(2)}, u32[]{:S(2)}) async-start(f32[32,4,128]{2,1,0:T(4,128)} %bitcast.11), calls=%async_computation.2 | async-start | bytes 131072 | tf_op jit(solution)/shard_map/all_to_all | solution.py:161
  118.4 290.3 %all-reduce.3.cloned.1.call-start = ((), (), s32[]{:S(2)}) async-start(), calls=%async_computation.3 | async-start | bytes 9175040 | tf_op jit(solution)/shard_map/psum | solution.py:174
  145.0 0.7 copy-start.10
  145.0 0.7 copy-start.12
  410.3 4.7 %copy-start.5 = (f32[512,128]{1,0:T(8,128)S(1)}, f32[512,128]{1,0:T(8,128)}, u32[]{:S(2)}) copy-start(f32[512,128]{1,0:T(8,128)} %get-tuple-element.34) | copy-start | bytes 786436
Sparse Core Ops, SparseCore 0:
  145.2 263.5 all-reduce.2
where the time goes:
time: 424 us; the launch traced here: 423 us
  waiting for transfers between devices  274 us (65%)
  blocking collectives  45.3 us (11%)
  starting transfers between devices  32.7 us (8%)
  matrix products  21.3 us (5%)
  local copies, waits for them, and re-layouts  21.1 us (5%)
  between operations  14.3 us (3%)
  other arithmetic  14.1 us (3%)
    psum x1, waiting for transfers between devices, on_device(): g_mix, g_in, g_out = lax.psum((g_mix, g_in, g_out), ('blk', 'dp'))  263 us
    all_gather x1, blocking collectives, on_device(): lax.all_gather(units, 'blk', axis=0, tiled=True)  26.6 us
    all_gather x1, blocking collectives, on_device(): all_totals = lax.all_gather(totals, 'blk', axis=0, tiled=True)  18.6 us
    all_to_all x1, starting transfers between devices, on_device(): lax.all_to_all(picked, 'dp', split_axis=0, concat_axis=0, tiled=True)  13.3 us
    all_to_all x1, starting transfers between devices, on_device(): lax.all_to_all(wanted, 'dp', split_axis=0, concat_axis=0, tiled=True)  11 us
    unnamed x33, local copies, waits for them, and re-layouts  8.52 us
  transfers between devices with their start and end apart: 4, of which 3 were waited for; matrix products, arithmetic and copies ran while one was open for 4% of the time, Pallas kernels for 0%

commit v1 on v0

v1 whole, which is shorter than its diff:
```python
import functools
import math

import jax
import jax.numpy as jnp
import ml_dtypes
import numpy as np
from jax import lax
from jax.experimental import pallas as pl
from jax.experimental.pallas import tpu as pltpu
from jax.sharding import PartitionSpec as P

SCALE = 10.0
MESH = pl.DeviceIdType.MESH
F32 = jnp.float32
BF16 = jnp.bfloat16

COUNT = 128
ANGLES = 64
LANES = 256
FREQS = 16
FILTERS = 128
FEATS = FREQS * FILTERS
HIDDEN = 512
EMBED = 128
PEERS = 32
CYCLE = 8
GROUP = CYCLE * COUNT
SLOT = 8
SMALL = 384
COEF = SCALE / COUNT


def block_table():
    angle = np.arange(ANGLES)
    freq = np.arange(FREQS)
    phase = np.mod(freq[None, :] * angle[:, None], ANGLES).astype(np.float32) * np.float32(
        2.0 * math.pi / ANGLES
    )
    table = np.concatenate([np.cos(phase), -np.sin(phase)], axis=1)
    wide = np.zeros((2 * FREQS, 8, 8, ANGLES), np.float32)
    for n in range(8):
        wide[:, n, n, :] = table.T
    return wide.reshape(2 * FREQS * 8, 8 * ANGLES).astype(ml_dtypes.bfloat16)


def dot(a, b):
    return jnp.dot(a, b, preferred_element_type=F32)


def dot_t(a, b):
    return lax.dot_general(a, b, (((1,), (1,)), ((), ())), preferred_element_type=F32)


def split(v):
    high = v.astype(BF16)
    return high, (v - high.astype(F32)).astype(BF16)


def iota(shape, dim):
    return lax.broadcasted_iota(jnp.int32, shape, dim)


def kernel(
    pdev_ref, prow_ref, table_hbm, wmix_hbm, win_hbm, wout_hbm, patches_hbm,
    loss_ref, big_ref, small_ref,
    patches, table, wmix, win, wout,
    spec, spec_t, real, imag, feat, normed, preact, hid_t, ngrad, mixg,
    group, ask_out, ask_in, row_out, row_in, back_out, back_in, tot_all,
    nt_own, nt_send, nt_sib, gp_own, gp_sib,
    pa, pb, ra1, rb1, pa2, pb2, ra2, rb2, pa3, pb3, ra3, rb3,
    sm, sm_sib, sm0, sz, sx, sy,
    load_sem, send_sem, recv_sem,
):
    blk = lax.axis_index("blk")
    dp = lax.axis_index("dp")
    y = blk // 2
    x = (blk % 2) * 2 + dp // 16
    z = (dp // 2) % 8
    core = dp % 2
    other = 1 - core

    def device(x_, y_, z_, c_):
        return (y_ * 2 + x_ // 2, ((x_ % 2) * 8 + z_) * 2 + c_)

    sibling = device(x, y, z, other)

    def dp_peer(i):
        quad = i // 4
        half = (quad + 1) // 2
        dz = 4 + half * (2 * (quad % 2) - 1)
        xl = (dp // 16 + 1 - (i % 4) // 2) % 2
        c = (core + 1 - i % 2) % 2
        return (xl * 8 + (z + dz) % 8) * 2 + c

    used = [0]
    started = []

    def remote(src, dst, to):
        k = used[0]
        used[0] += 1
        copy = pltpu.make_async_remote_copy(
            src_ref=src, dst_ref=dst, send_sem=send_sem.at[k], recv_sem=recv_sem.at[k],
            device_id=to, device_id_type=MESH,
        )
        copy.start()
        started.append(copy)
        return copy

    def spread(src, dst):
        k = used[0]
        used[0] += 1
        mine = pl.multiple_of(dp * SLOT, SLOT)

        def send(i, carry):
            p = dp_peer(i)
            pltpu.make_async_remote_copy(
                src_ref=src.at[pl.ds(pl.multiple_of(p * SLOT, SLOT), SLOT)],
                dst_ref=dst.at[pl.ds(mine, SLOT)],
                send_sem=send_sem.at[k], recv_sem=recv_sem.at[k],
                device_id=(blk, p), device_id_type=MESH,
            ).start()
            return carry

        lax.fori_loop(0, PEERS - 1, send, 0)
        dst[pl.ds(mine, SLOT), :] = src[pl.ds(mine, SLOT), :]
        rows = pl.ds(0, (PEERS - 1) * SLOT)
        whole = pltpu.make_async_remote_copy(
            src_ref=src.at[rows], dst_ref=dst.at[rows], send_sem=send_sem.at[k],
            recv_sem=recv_sem.at[k], device_id=(blk, dp_peer(0)), device_id_type=MESH,
        )
        started.append(whole)
        return whole

    def to_group(ref, rows):
        k = used[0]
        used[0] += 1
        mine = pl.ds(pl.multiple_of(blk * rows, rows), rows)
        for step in (5, 4, 3, 2, 1, 6, 7):
            pltpu.make_async_remote_copy(
                src_ref=ref.at[mine], dst_ref=ref.at[mine],
                send_sem=send_sem.at[k], recv_sem=recv_sem.at[k],
                device_id=((blk + step) % CYCLE, dp), device_id_type=MESH,
            ).start()
        span = pl.ds(0, (CYCLE - 1) * rows)
        whole = pltpu.make_async_remote_copy(
            src_ref=ref.at[span], dst_ref=ref.at[span], send_sem=send_sem.at[k],
            recv_sem=recv_sem.at[k], device_id=((blk + 1) % CYCLE, dp), device_id_type=MESH,
        )
        started.append(whole)
        return whole

    chunk = 1024
    loads = [pltpu.make_async_copy(table_hbm, table, load_sem.at[0])]
    for g in range(8):
        rows = pl.ds(g * chunk, chunk)
        loads.append(pltpu.make_async_copy(patches_hbm.at[rows], patches.at[rows], load_sem.at[1 + g]))
    loads.append(pltpu.make_async_copy(wmix_hbm, wmix, load_sem.at[9]))
    loads.append(pltpu.make_async_copy(win_hbm, win, load_sem.at[10]))
    loads.append(pltpu.make_async_copy(wout_hbm, wout, load_sem.at[11]))
    for load in loads:
        load.start()

    barrier = pltpu.get_barrier_semaphore()

    def greet(i, carry):
        pl.semaphore_signal(barrier, inc=1, device_id=(blk, dp_peer(i)), device_id_type=MESH)
        return carry

    lax.fori_loop(0, PEERS - 1, greet, 0)
    for step in range(1, CYCLE):
        pl.semaphore_signal(barrier, inc=1, device_id=((blk + step) % CYCLE, dp), device_id_type=MESH)
    pl.semaphore_signal(barrier, inc=1, device_id=device(3 - x, y, z, core), device_id_type=MESH)

    lane = iota((COUNT, COUNT), 1)
    row = iota((COUNT, COUNT), 0)
    dev_lane = jnp.broadcast_to(pdev_ref[...], (COUNT, COUNT))
    dev_row = dev_lane.astype(F32).T.astype(jnp.int32)
    same = dev_lane == dev_row
    rank_lane = jnp.sum(jnp.where(same & (row < lane), 1.0, 0.0), axis=0, keepdims=True)
    rank_row = jnp.sum(jnp.where(same & (lane < row), 1.0, 0.0), axis=1, keepdims=True)
    place_lane = pdev_ref[...] * SLOT + rank_lane.astype(jnp.int32)
    place_row = dev_row[:, :1] * SLOT + rank_row.astype(jnp.int32)
    to_slot = jnp.where(
        iota((PEERS * SLOT, COUNT), 0) == place_lane, 1.0, 0.0
    ).astype(BF16)
    from_slot = jnp.where(
        iota((COUNT, PEERS * SLOT), 1) == place_row, 1.0, 0.0
    ).astype(BF16)
    prow = jnp.broadcast_to(prow_ref[...], (COUNT, COUNT)).astype(F32).T.astype(BF16)
    ask_out[...] = dot(to_slot, prow)

    pl.semaphore_wait(barrier, PEERS - 1 + CYCLE - 1 + 1)
    asked = spread(ask_out, ask_in)

    loads[0].wait()
    bank = table[...]
    for g in range(8):
        loads[1 + g].wait()
        low = dot(bank, patches[g * chunk : g * chunk + 512, :])
        high = dot(bank, patches[g * chunk + 512 : (g + 1) * chunk, :])
        for k in range(2 * FREQS):
            part = jnp.concatenate([low[k * 8 : k * 8 + 8], high[k * 8 : k * 8 + 8]], axis=0)
            spec[k * COUNT + g * 16 : k * COUNT + g * 16 + 16, :] = part.astype(BF16)

    loads[9].wait()
    total = jnp.zeros((COUNT, 1), F32)
    for k in range(0, FREQS, 4):
        rows = slice(k * COUNT, (k + 4) * COUNT)
        re = dot(spec[rows, :], wmix[...])
        im = dot(spec[(FREQS + k) * COUNT : (FREQS + k + 4) * COUNT, :], wmix[...])
        real[rows, :] = re
        imag[rows, :] = im
        value = jnp.log1p(re * re + im * im)
        acc = jnp.zeros((COUNT, FILTERS), F32)
        for i in range(4):
            piece = value[i * COUNT : (i + 1) * COUNT]
            feat[:, (k + i) * FILTERS : (k + i + 1) * FILTERS] = piece
            acc = acc + piece
        total = total + jnp.sum(acc, axis=1, keepdims=True)
    mean = total * (1.0 / FEATS)
    acc = jnp.zeros((COUNT, FILTERS), F32)
    for k in range(FREQS):
        off = feat[:, k * FILTERS : (k + 1) * FILTERS] - mean
        acc = acc + off * off
    rscale = lax.rsqrt(jnp.sum(acc, axis=1, keepdims=True) * (1.0 / FEATS) + 1e-05)
    for k in range(FREQS):
        cols = slice(k * FILTERS, (k + 1) * FILTERS)
        hat = (feat[:, cols] - mean) * rscale
        feat[:, cols] = hat
        normed[:, cols] = hat.astype(BF16)

    loads[10].wait()
    pre = dot(normed[...], win[...])
    preact[...] = pre
    hidden = (pre * jax.nn.sigmoid(pre)).astype(BF16)
    loads[11].wait()
    raw = dot(hidden, wout[...])
    norms = jnp.sqrt(jnp.sum(raw * raw, axis=1, keepdims=True) + 1e-06)
    unit32 = raw / norms
    units = unit32.astype(BF16)
    group[pl.ds(pl.multiple_of(blk * COUNT, COUNT), COUNT), :] = units
    gathered = to_group(group, COUNT)

    asked.wait_recv()
    wanted = ask_in[...]
    valid = iota((PEERS * SLOT, COUNT), 0) % SLOT < SLOT // 2
    pick32 = jnp.where(
        valid & (wanted == iota((PEERS * SLOT, COUNT), 1).astype(F32)), 1.0, 0.0
    )
    pick = pick32.astype(BF16)
    row_out[...] = dot(pick, units)
    returned = spread(row_out, row_in)

    unpick = pick32.T.astype(BF16)
    base = core * (FEATS // 2)
    for k in range(8):
        cols = pl.ds(pl.multiple_of((1 - core) * (FEATS // 2) + k * FILTERS, FILTERS), FILTERS)
        nt_send[k * FILTERS : (k + 1) * FILTERS, :] = normed[:, cols].T
    factor = remote(nt_send, nt_sib, sibling)
    for k in range(8):
        cols = pl.ds(pl.multiple_of(base + k * FILTERS, FILTERS), FILTERS)
        nt_own[k * FILTERS : (k + 1) * FILTERS, :] = normed[:, cols].T
    hid_t[...] = hidden.T
    for k in range(2 * FREQS):
        spec_t[:, k * COUNT : (k + 1) * COUNT] = spec[k * COUNT : (k + 1) * COUNT, :].T

    gathered.wait_recv()
    keys = group[...]
    scores = SCALE * dot_t(units, keys)
    self_lane = blk * COUNT + iota((COUNT, GROUP), 0)
    expo = jnp.where(iota((COUNT, GROUP), 1) == self_lane, 0.0, jnp.exp(scores))
    zneg = jnp.sum(expo, axis=1, keepdims=True)
    numer = dot(expo.astype(BF16), keys)

    returned.wait_recv()
    positive = dot(from_slot, row_in[...].astype(BF16))
    own = units.astype(F32)
    spos = SCALE * jnp.sum(own * positive, axis=1, keepdims=True)
    epos = jnp.exp(spos)
    totals = epos + zneg
    tot_lane = jnp.broadcast_to(totals, (COUNT, COUNT)).T
    tot_all[pl.ds(pl.multiple_of(blk * SLOT, SLOT), SLOT), :] = tot_lane[:SLOT]
    tots = to_group(tot_all, SLOT)
    away = COEF * (epos / totals - 1.0)
    high, low = split(away * own)
    back_out[...] = dot(to_slot, high) + dot(to_slot, low)
    backs = spread(back_out, back_in)
    spos_lane = jnp.broadcast_to(spos, (COUNT, COUNT)).T
    loss_ref[...] = (jnp.log(tot_lane) - spos_lane)[:1]
    grad_units = away * positive + COEF * (numer / totals)

    tots.wait_recv()
    inverse = jnp.concatenate(
        [1.0 / tot_all[b * SLOT : b * SLOT + 1, :] for b in range(CYCLE)], axis=1
    )
    keyterm = dot((expo * inverse).astype(BF16), keys)
    grad_units = grad_units + COEF * keyterm
    backs.wait_recv()
    high, low = split(back_in[...])
    grad_units = grad_units + (dot(unpick, high) + dot(unpick, low))

    grad_raw = (
        (grad_units - unit32 * jnp.sum(unit32 * grad_units, axis=1, keepdims=True)) / norms
    ).astype(BF16)
    grad_hid = dot_t(grad_raw, wout[...])
    pre = preact[...]
    sigm = jax.nn.sigmoid(pre)
    grad_pre = (grad_hid * sigm * (1.0 + pre * (1.0 - sigm))).astype(BF16)
    gp_own[...] = grad_pre
    sent = remote(gp_own, gp_sib, sibling)
    g_out = dot(hid_t[...], grad_raw)
    sm[0, 0:256, :] = g_out[:256]
    sm[1, 0:256, :] = g_out[256:]
    ngrad[...] = dot_t(grad_pre, win[...])

    factor.wait_recv()
    sent.wait_recv()
    right = jnp.concatenate([gp_own[...], gp_sib[...]], axis=0)
    for i in range(4):
        rows = slice(i * 256, (i + 1) * 256)
        prod = dot(jnp.concatenate([nt_own[rows, :], nt_sib[rows, :]], axis=1), right).astype(BF16)
        pa[i * 256 : (i + 1) * 256, :] = prod[:, 0:128]
        pa[1024 + i * 256 : 1024 + (i + 1) * 256, :] = prod[:, 128:256]
        pb[i * 256 : (i + 1) * 256, :] = prod[:, 256:384]
        pb[1024 + i * 256 : 1024 + (i + 1) * 256, :] = prod[:, 384:512]

    def x_peer(k):
        return device((x + k) % 4, y, z, core)

    def y_peer(k):
        return device(x, (y + k) % 4, z, core)

    def z_peer(k):
        return device(x, y, (z + k) % 8, core)

    def piece(at, rows):
        return pl.ds(pl.multiple_of(at * rows, rows), rows)

    a1 = {}
    b1 = {}
    for k in (2, 1, 3):
        a1[k] = remote(pa.at[piece((x + k) % 4, 512)], ra1.at[k - 1], x_peer(k))
        b1[k] = remote(pb.at[piece((y + k) % 4, 512)], rb1.at[k - 1], y_peer(k))

    acc = jnp.zeros((COUNT, FILTERS), F32)
    acc_hat = jnp.zeros((COUNT, FILTERS), F32)
    for k in range(FREQS):
        cols = slice(k * FILTERS, (k + 1) * FILTERS)
        ng = ngrad[:, cols]
        acc = acc + ng
        acc_hat = acc_hat + ng * feat[:, cols]
    mean_ng = jnp.sum(acc, axis=1, keepdims=True) * (1.0 / FEATS)
    mean_hat = jnp.sum(acc_hat, axis=1, keepdims=True) * (1.0 / FEATS)
    for k in range(FREQS):
        cols = slice(k * FILTERS, (k + 1) * FILTERS)
        rows = slice(k * COUNT, (k + 1) * COUNT)
        re = real[rows, :]
        im = imag[rows, :]
        grad_feat = rscale * (ngrad[:, cols] - mean_ng - feat[:, cols] * mean_hat)
        grad_pow = 2.0 * grad_feat / (1.0 + (re * re + im * im))
        mixg[rows, :] = (re * grad_pow).astype(BF16)
        mixg[(FREQS + k) * COUNT : (FREQS + k + 1) * COUNT, :] = (im * grad_pow).astype(BF16)
    g_mix = dot(spec_t[...], mixg[...])
    sm[0, 256:384, :] = g_mix[:128]
    sm[1, 256:384, :] = g_mix[128:]
    halves = remote(sm.at[other], sm_sib, sibling)

    def add(own_part, got, copies):
        value = own_part.astype(F32)
        for k in sorted(copies):
            copies[k].wait_recv()
            value = value + got[k - 1].astype(F32)
        return value.astype(BF16)

    pa2[...] = add(pa[piece(x, 512), :], ra1, a1)
    a2 = {k: remote(pa2.at[piece((y + k) % 4, 128)], ra2.at[k - 1], y_peer(k)) for k in (2, 1, 3)}
    pb2[...] = add(pb[piece(y, 512), :], rb1, b1)
    b2 = {k: remote(pb2.at[piece((x + k) % 4, 128)], rb2.at[k - 1], x_peer(k)) for k in (2, 1, 3)}

    halves.wait_recv()
    sm0[...] = (sm[core] + sm_sib[...]).astype(BF16)
    far = (4, 3, 5, 2, 6, 1, 7)
    s1 = {k: remote(sm0.at[piece((z + k) % 8, 48)], sz.at[k - 1], z_peer(k)) for k in far}

    pa3[...] = add(pa2[piece(y, 128), :], ra2, a2)
    a3 = {k: remote(pa3.at[piece((z + k) % 8, 16)], ra3.at[k - 1], z_peer(k)) for k in far}
    pb3[...] = add(pb2[piece(x, 128), :], rb2, b2)
    b3 = {k: remote(pb3.at[piece((z + k) % 8, 16)], rb3.at[k - 1], z_peer(k)) for k in far}

    sx[x] = add(sm0[piece(z, 48), :], sz, s1)
    s2 = [remote(sx.at[x], sx.at[x], x_peer(k)) for k in (2, 1, 3)]

    a_own = x * 512 + y * 128
    b_own = y * 512 + x * 128

    def span(at, rows):
        return pl.ds(pl.multiple_of(at, rows), rows)

    big_ref[core, 0, span(a_own + z * 16, 16), :] = add(pa3[piece(z, 16), :], ra3, a3)
    here = big_ref.at[core, 0, span(a_own + z * 16, 16)]
    a4 = [remote(here, here, z_peer(k)) for k in far]
    big_ref[core, 1, span(b_own + z * 16, 16), :] = add(pb3[piece(z, 16), :], rb3, b3)
    here_b = big_ref.at[core, 1, span(b_own + z * 16, 16)]
    b4 = [remote(here_b, here_b, z_peer(k)) for k in far]

    def four(ref):
        value = ref[0].astype(F32)
        for i in range(1, 4):
            value = value + ref[i].astype(F32)
        return value.astype(BF16)

    for copy in s2:
        copy.wait_recv()
    sy[y] = four(sx)
    s3 = [remote(sy.at[y], sy.at[y], y_peer(k)) for k in (2, 1, 3)]

    for copy in a4:
        copy.wait_recv()
    mid = big_ref.at[core, 0, span(a_own, 128)]
    a5 = [remote(mid, mid, y_peer(k)) for k in (2, 1, 3)]
    for copy in b4:
        copy.wait_recv()
    mid_b = big_ref.at[core, 1, span(b_own, 128)]
    b5 = [remote(mid_b, mid_b, x_peer(k)) for k in (2, 1, 3)]

    for copy in s3:
        copy.wait_recv()
    small_ref[core, piece(z, 48), :] = four(sy)
    bit = small_ref.at[core, piece(z, 48)]
    s4 = [remote(bit, bit, z_peer(k)) for k in far]

    for copy in a5:
        copy.wait_recv()
    quarter = big_ref.at[core, 0, piece(x, 512)]
    order = (2, 1, 3)
    a6 = [remote(quarter, quarter, x_peer(k)) for k in order]
    for copy in b5:
        copy.wait_recv()
    quarter_b = big_ref.at[core, 1, piece(y, 512)]
    b6 = [remote(quarter_b, quarter_b, y_peer(k)) for k in order]

    last = [remote(quarter, quarter, sibling), remote(quarter_b, quarter_b, sibling)]
    for copy in s4:
        copy.wait_recv()
    last.append(remote(small_ref.at[core], small_ref.at[core], sibling))
    for i in (1, 2, 0):
        k = order[i]
        a6[i].wait_recv()
        got = big_ref.at[core, 0, piece((x + 4 - k) % 4, 512)]
        last.append(remote(got, got, sibling))
        b6[i].wait_recv()
        got_b = big_ref.at[core, 1, piece((y + 4 - k) % 4, 512)]
        last.append(remote(got_b, got_b, sibling))
    for copy in last:
        copy.wait_recv()
    for copy in started:
        copy.wait_send()


N_SEM = 140


def widen(big_ref, small_ref, in_ref, out_ref, mix_ref):
    for j in range(4):
        in_ref[:, j * 128 : (j + 1) * 128] = big_ref[0, j // 2, j % 2].astype(F32)

    @pl.when((pl.program_id(0) == 0) & (pl.program_id(1) == 0))
    def _():
        for h in range(2):
            out_ref[h * 256 : (h + 1) * 256, :] = small_ref[h, 0:256].astype(F32)
            mix_ref[h * 128 : (h + 1) * 128, :] = small_ref[h, 256:384].astype(F32)


def on_device(patches, w_mix, w_in, w_out, partner_dev, partner_row):
    vmem = pltpu.VMEM
    any_spec = pl.BlockSpec(memory_space=pl.ANY)
    vmem_spec = pl.BlockSpec(memory_space=pltpu.VMEM)
    scratch = [
        vmem((COUNT * ANGLES, LANES), BF16),
        vmem((256, 512), BF16),
        vmem((LANES, FILTERS), BF16),
        vmem((FEATS, HIDDEN), BF16),
        vmem((HIDDEN, EMBED), BF16),
        vmem((2 * FREQS * COUNT, LANES), BF16),
        vmem((LANES, 2 * FREQS * COUNT), BF16),
        vmem((FREQS * COUNT, FILTERS), F32),
        vmem((FREQS * COUNT, FILTERS), F32),
        vmem((COUNT, FEATS), F32),
        vmem((COUNT, FEATS), BF16),
        vmem((COUNT, HIDDEN), F32),
        vmem((HIDDEN, COUNT), BF16),
        vmem((COUNT, FEATS), F32),
        vmem((2 * FREQS * COUNT, FILTERS), BF16),
        vmem((GROUP, EMBED), BF16),
        vmem((PEERS * SLOT, COUNT), F32),
        vmem((PEERS * SLOT, COUNT), F32),
        vmem((PEERS * SLOT, EMBED), F32),
        vmem((PEERS * SLOT, EMBED), F32),
        vmem((PEERS * SLOT, EMBED), F32),
        vmem((PEERS * SLOT, EMBED), F32),
        vmem((CYCLE * SLOT, COUNT), F32),
        vmem((FEATS // 2, COUNT), BF16),
        vmem((FEATS // 2, COUNT), BF16),
        vmem((FEATS // 2, COUNT), BF16),
        vmem((COUNT, HIDDEN), BF16),
        vmem((COUNT, HIDDEN), BF16),
        vmem((2048, 128), BF16),
        vmem((2048, 128), BF16),
        vmem((3, 512, 128), BF16),
        vmem((3, 512, 128), BF16),
        vmem((512, 128), BF16),
        vmem((512, 128), BF16),
        vmem((3, 128, 128), BF16),
        vmem((3, 128, 128), BF16),
        vmem((128, 128), BF16),
        vmem((128, 128), BF16),
        vmem((7, 16, 128), BF16),
        vmem((7, 16, 128), BF16),
        vmem((2, SMALL, 128), F32),
        vmem((SMALL, 128), F32),
        vmem((SMALL, 128), BF16),
        vmem((7, 48, 128), BF16),
        vmem((4, 48, 128), BF16),
        vmem((4, 48, 128), BF16),
        pltpu.SemaphoreType.DMA((12,)),
        pltpu.SemaphoreType.DMA((N_SEM,)),
        pltpu.SemaphoreType.DMA((N_SEM,)),
    ]
    loss, big, small = pl.pallas_call(
        kernel,
        name="contrastive_step",
        out_shape=(
            jax.ShapeDtypeStruct((1, COUNT), F32),
            jax.ShapeDtypeStruct((2, 2, 2048, 128), BF16),
            jax.ShapeDtypeStruct((2, SMALL, 128), BF16),
        ),
        in_specs=[vmem_spec, vmem_spec] + [any_spec] * 5,
        out_specs=(vmem_spec, vmem_spec, vmem_spec),
        scratch_shapes=scratch,
        compiler_params=pltpu.CompilerParams(
            collective_id=0, has_side_effects=True, vmem_limit_bytes=56 * 2**20
        ),
    )(
        partner_dev.reshape(1, COUNT),
        partner_row.reshape(1, COUNT),
        jnp.asarray(block_table()),
        w_mix,
        w_in,
        w_out,
        patches.reshape(COUNT * ANGLES, LANES),
    )
    rows = 256
    steps = FEATS // 2 // rows
    g_in, g_out, g_mix = pl.pallas_call(
        widen,
        name="widen",
        grid=(2, steps),
        out_shape=(
            jax.ShapeDtypeStruct((FEATS, HIDDEN), F32),
            jax.ShapeDtypeStruct((HIDDEN, EMBED), F32),
            jax.ShapeDtypeStruct((LANES, FILTERS), F32),
        ),
        in_specs=[
            pl.BlockSpec((1, 2, 2, rows, 128), lambda c, i: (c, 0, 0, i, 0)),
            pl.BlockSpec((2, SMALL, 128), lambda c, i: (0, 0, 0)),
        ],
        out_specs=(
            pl.BlockSpec((rows, HIDDEN), lambda c, i: (c * steps + i, 0)),
            pl.BlockSpec((HIDDEN, EMBED), lambda c, i: (0, 0)),
            pl.BlockSpec((LANES, FILTERS), lambda c, i: (0, 0)),
        ),
    )(big.reshape(2, 2, 2, FEATS // 2, 128), small)
    return (loss.reshape(COUNT), g_mix, g_in, g_out)


def solution(mesh):
    placed = (P(("blk", "dp"), None, None), P(), P(), P(), P(("blk", "dp")), P(("blk", "dp")))
    return jax.shard_map(
        on_device,
        mesh=mesh,
        in_specs=placed,
        out_specs=(P(("blk", "dp")), P(), P(), P()),
        check_vma=False,
    )
```

time: 424 us -> 79.9 us (0.19)
  waiting for transfers between devices: 274 us -> 0 us
  Pallas kernels: 0 us -> 77.9 us
  blocking collectives: 45.3 us -> 0 us
  starting transfers between devices: 32.7 us -> 0 us
  matrix products: 21.3 us -> 0 us
  local copies, waits for them, and re-layouts: 21.1 us -> 1.13 us
  other arithmetic: 14.1 us -> 0 us
  between operations: 14.3 us -> 0.64 us
    psum x1 -> x0, waiting for transfers between devices: 263 us -> none  [on_device(): g_mix, g_in, g_out = lax.psum((g_mix, g_in, g_out), ('blk', 'dp'))]
    pallas_call x0 -> x2, Pallas kernels: none -> 77.9 us  [the longest x1 71.5 us: on_device(): pl.pallas_call(kernel, name='contrastive_step', out_shape=(jax.ShapeDtype...]
    all_gather x2 -> x0, blocking collectives: 45.3 us -> none  [the longest x1 26.6 us: on_device(): lax.all_gather(units, 'blk', axis=0, tiled=True)]
    all_to_all x3 -> x0, starting transfers between devices: 32.7 us -> none  [the longest x1 13.3 us: on_device(): lax.all_to_all(picked, 'dp', split_axis=0, concat_axis=0, tiled=True)]
    dot_general x12 -> x0, matrix products: 21.3 us -> none  [the longest x1 3.26 us: back_lower(): jnp.dot(spec.reshape(-1, lanes).T, grad_mixed.reshape(-1, grad_mixed.shap...]
    all_to_all x3 -> x0, waiting for transfers between devices: 11.1 us -> none  [the longest x1 7.35 us: on_device(): lax.all_to_all(picked, 'dp', split_axis=0, concat_axis=0, tiled=True)]
    unnamed x33 -> x1, local copies, waits for them, and re-layouts: 8.52 us -> 1.13 us
    sort x2 -> x0, other arithmetic: 5.87 us -> none  [the longest x1 3.33 us: on_device(): sorted_positions = jnp.argsort(partner_dev, stable=True)]
  transfers between devices with their start and end apart: 4 -> 0, of which waited for: 3 -> 0; matrix products, arithmetic and copies ran while one was open for 4% -> 0% of each run, Pallas kernels for 0% -> 0%
where the time goes in v1:
time: 79.9 us; the launch traced here: 79.6 us
  Pallas kernels  77.9 us (97%)
  local copies, waits for them, and re-layouts  1.13 us (1%)
    pallas_call x1, Pallas kernels, on_device(): pl.pallas_call(kernel, name='contrastive_step', out_shape=(jax.ShapeDtype...  71.5 us
    pallas_call x1, Pallas kernels, on_device(): pl.pallas_call(widen, name='widen', grid=(2, steps), out_shape=(jax.Shape...  6.36 us

profile of v1, /device:TPU:1, one launch (start us, length us, event | category | flops | bytes accessed | tf_op | source)
XLA Modules:
  0.0 79.6 jit_solution(4159231899322090532)
XLA Ops:
  0.6 71.5 %contrastive_step.1 = (f32[1,128]{1,0:T(1,128)}, bf16[2,2,2048,128]{3,2,1,0:T(8,128)(2,1)}, bf16[2,384,128]{2,1,0:T(8,128)(2,1)}) custom-call(s32[1,128]{1,0:T(1,128)} %bitcast.7, s32[1,128]{1,0:T(1,128)} %bitcast.8, bf16[256,512]{1,0:T(8,128)(2,1)} %constant.2.clone.table_hbm, bf16[256,128]{1,0:T(8,128)(2,1)} %wmix_hbm.1, bf16[2048,512]{1,0:T(8,128)(2,1)} %win_hbm.1, ...), custom_call_target="tpu_custom_call" | custom-call | tf_op jit(solution)/shard_map/contrastive_step/pallas_call | solution.py:530
  72.2 6.4 %widen.1 = (f32[2048,512]{1,0:T(8,128)}, f32[512,128]{1,0:T(8,128)}, f32[256,128]{1,0:T(8,128)}) custom-call(bf16[2,2,2,1024,128]{4,3,2,1,0:T(8,128)(2,1)} %bitcast.6, bf16[2,384,128]{2,1,0:T(8,128)(2,1)} %get-tuple-element.12.small_ref), custom_call_target="tpu_custom_call" | custom-call | tf_op jit(solution)/shard_map/widen/pallas_call | solution.py:555
  78.5 1.1 %copy.12 = f32[128]{0:T(128)} copy(f32[128]{0:T(128)} %bitcast.9) | data formatting | bytes 1024

commit v2 on v1

--- a/solution.py
+++ b/solution.py
@@ -26,7 +26,8 @@
 PEERS = 32
 CYCLE = 8
 GROUP = CYCLE * COUNT
-SLOT = 8
+SLOT = COUNT // PEERS
+TILE = 8
 SMALL = 384
 COEF = SCALE / COUNT
 
@@ -70,7 +71,8 @@
     nt_own, nt_send, nt_sib, gp_own, gp_sib,
     pa, pb, ra1, rb1, pa2, pb2, ra2, rb2, pa3, pb3, ra3, rb3,
     sm, sm_sib, sm0, sz, sx, sy,
-    load_sem, send_sem, recv_sem,
+    big, small, loss,
+    load_sem, keep_sem, send_sem, recv_sem,
 ):
     blk = lax.axis_index("blk")
     dp = lax.axis_index("dp")
@@ -107,30 +109,33 @@
         started.append(copy)
         return copy
 
-    def spread(src, dst):
+    def spread(value, src, dst):
         k = used[0]
         used[0] += 1
-        mine = pl.multiple_of(dp * SLOT, SLOT)
+        for p in range(PEERS):
+            src[p] = value[p * SLOT : (p + 1) * SLOT]
 
         def send(i, carry):
             p = dp_peer(i)
             pltpu.make_async_remote_copy(
-                src_ref=src.at[pl.ds(pl.multiple_of(p * SLOT, SLOT), SLOT)],
-                dst_ref=dst.at[pl.ds(mine, SLOT)],
+                src_ref=src.at[p], dst_ref=dst.at[dp],
                 send_sem=send_sem.at[k], recv_sem=recv_sem.at[k],
                 device_id=(blk, p), device_id_type=MESH,
             ).start()
             return carry
 
         lax.fori_loop(0, PEERS - 1, send, 0)
-        dst[pl.ds(mine, SLOT), :] = src[pl.ds(mine, SLOT), :]
-        rows = pl.ds(0, (PEERS - 1) * SLOT)
+        dst[dp] = src[dp]
+        rows = pl.ds(0, PEERS - 1)
         whole = pltpu.make_async_remote_copy(
             src_ref=src.at[rows], dst_ref=dst.at[rows], send_sem=send_sem.at[k],
             recv_sem=recv_sem.at[k], device_id=(blk, dp_peer(0)), device_id_type=MESH,
         )
         started.append(whole)
         return whole
+
+    def flat(ref):
+        return jnp.concatenate([ref[p] for p in range(PEERS)], axis=0)
 
     def to_group(ref, rows):
         k = used[0]
@@ -150,6 +155,13 @@
         started.append(whole)
         return whole
 
+    kept = []
+
+    def keep(src, dst):
+        copy = pltpu.make_async_copy(src, dst, keep_sem.at[len(kept)])
+        copy.start()
+        kept.append(copy)
+
     chunk = 1024
     loads = [pltpu.make_async_copy(table_hbm, table, load_sem.at[0])]
     for g in range(8):
@@ -188,10 +200,7 @@
         iota((COUNT, PEERS * SLOT), 1) == place_row, 1.0, 0.0
     ).astype(BF16)
     prow = jnp.broadcast_to(prow_ref[...], (COUNT, COUNT)).astype(F32).T.astype(BF16)
-    ask_out[...] = dot(to_slot, prow)
-
-    pl.semaphore_wait(barrier, PEERS - 1 + CYCLE - 1 + 1)
-    asked = spread(ask_out, ask_in)
+    ask = dot(to_slot, prow)
 
     loads[0].wait()
     bank = table[...]
@@ -202,6 +211,9 @@
         for k in range(2 * FREQS):
             part = jnp.concatenate([low[k * 8 : k * 8 + 8], high[k * 8 : k * 8 + 8]], axis=0)
             spec[k * COUNT + g * 16 : k * COUNT + g * 16 + 16, :] = part.astype(BF16)
+
+    pl.semaphore_wait(barrier, PEERS - 1 + CYCLE - 1 + 1)
+    asked = spread(ask, ask_out, ask_in)
 
     loads[9].wait()
     total = jnp.zeros((COUNT, 1), F32)
@@ -243,14 +255,8 @@
     gathered = to_group(group, COUNT)
 
     asked.wait_recv()
-    wanted = ask_in[...]
-    valid = iota((PEERS * SLOT, COUNT), 0) % SLOT < SLOT // 2
-    pick32 = jnp.where(
-        valid & (wanted == iota((PEERS * SLOT, COUNT), 1).astype(F32)), 1.0, 0.0
-    )
-    pick = pick32.astype(BF16)
-    row_out[...] = dot(pick, units)
-    returned = spread(row_out, row_in)
+    pick32 = jnp.where(flat(ask_in) == lane.astype(F32), 1.0, 0.0)
+    returned = spread(dot(pick32.astype(BF16), units), row_out, row_in)
 
     unpick = pick32.T.astype(BF16)
     base = core * (FEATS // 2)
@@ -274,30 +280,30 @@
     numer = dot(expo.astype(BF16), keys)
 
     returned.wait_recv()
-    positive = dot(from_slot, row_in[...].astype(BF16))
+    positive = dot(from_slot, flat(row_in).astype(BF16))
     own = units.astype(F32)
     spos = SCALE * jnp.sum(own * positive, axis=1, keepdims=True)
     epos = jnp.exp(spos)
     totals = epos + zneg
     tot_lane = jnp.broadcast_to(totals, (COUNT, COUNT)).T
-    tot_all[pl.ds(pl.multiple_of(blk * SLOT, SLOT), SLOT), :] = tot_lane[:SLOT]
-    tots = to_group(tot_all, SLOT)
+    tot_all[pl.ds(pl.multiple_of(blk * TILE, TILE), TILE), :] = tot_lane[:TILE]
+    tots = to_group(tot_all, TILE)
     away = COEF * (epos / totals - 1.0)
     high, low = split(away * own)
-    back_out[...] = dot(to_slot, high) + dot(to_slot, low)
-    backs = spread(back_out, back_in)
+    backs = spread(dot(to_slot, high) + dot(to_slot, low), back_out, back_in)
     spos_lane = jnp.broadcast_to(spos, (COUNT, COUNT)).T
-    loss_ref[...] = (jnp.log(tot_lane) - spos_lane)[:1]
+    loss[...] = (jnp.log(tot_lane) - spos_lane)[:1]
+    keep(loss, loss_ref)
     grad_units = away * positive + COEF * (numer / totals)
 
     tots.wait_recv()
     inverse = jnp.concatenate(
-        [1.0 / tot_all[b * SLOT : b * SLOT + 1, :] for b in range(CYCLE)], axis=1
+        [1.0 / tot_all[b * TILE : b * TILE + 1, :] for b in range(CYCLE)], axis=1
     )
     keyterm = dot((expo * inverse).astype(BF16), keys)
     grad_units = grad_units + COEF * keyterm
     backs.wait_recv()
-    high, low = split(back_in[...])
+    high, low = split(flat(back_in))
     grad_units = grad_units + (dot(unpick, high) + dot(unpick, low))
 
     grad_raw = (
@@ -319,11 +325,9 @@
     right = jnp.concatenate([gp_own[...], gp_sib[...]], axis=0)
     for i in range(4):
         rows = slice(i * 256, (i + 1) * 256)
-        prod = dot(jnp.concatenate([nt_own[rows, :], nt_sib[rows, :]], axis=1), right).astype(BF16)
-        pa[i * 256 : (i + 1) * 256, :] = prod[:, 0:128]
-        pa[1024 + i * 256 : 1024 + (i + 1) * 256, :] = prod[:, 128:256]
-        pb[i * 256 : (i + 1) * 256, :] = prod[:, 256:384]
-        pb[1024 + i * 256 : 1024 + (i + 1) * 256, :] = prod[:, 384:512]
+        prod = dot(jnp.concatenate([nt_own[rows, :], nt_sib[rows, :]], axis=1), right)
+        to = pa if i < 2 else pb
+        to[(i % 2) * 256 : (i % 2 + 1) * 256, :] = prod.astype(BF16)
 
     def x_peer(k):
         return device((x + k) % 4, y, z, core)
@@ -337,11 +341,24 @@
     def piece(at, rows):
         return pl.ds(pl.multiple_of(at * rows, rows), rows)
 
-    a1 = {}
-    b1 = {}
-    for k in (2, 1, 3):
-        a1[k] = remote(pa.at[piece((x + k) % 4, 512)], ra1.at[k - 1], x_peer(k))
-        b1[k] = remote(pb.at[piece((y + k) % 4, 512)], rb1.at[k - 1], y_peer(k))
+    def cell(at):
+        return (piece(at // 4, 16), piece(at % 4, 128))
+
+    parts = (
+        (pa, ra1, pa2, ra2, pa3, ra3, x, y, x_peer, y_peer),
+        (pb, rb1, pb2, rb2, pb3, rb3, y, x, y_peer, x_peer),
+    )
+    far4 = (2, 1, 3)
+    far = (4, 3, 5, 2, 6, 1, 7)
+    step1 = ({}, {})
+    for j in (2, 1, 3, 0):
+        for n, (src, got, _, _, _, _, u, v, u_peer, _) in enumerate(parts):
+            for k in far4:
+                step1[n][j, k] = remote(
+                    src.at[piece((u + k) % 4 * 4 + (v + j) % 4, 32)],
+                    got.at[k - 1, piece((v + j) % 4, 32)],
+                    u_peer(k),
+                )
 
     acc = jnp.zeros((COUNT, FILTERS), F32)
     acc_hat = jnp.zeros((COUNT, FILTERS), F32)
@@ -373,36 +390,41 @@
             value = value + got[k - 1].astype(F32)
         return value.astype(BF16)
 
-    pa2[...] = add(pa[piece(x, 512), :], ra1, a1)
-    a2 = {k: remote(pa2.at[piece((y + k) % 4, 128)], ra2.at[k - 1], y_peer(k)) for k in (2, 1, 3)}
-    pb2[...] = add(pb[piece(y, 512), :], rb1, b1)
-    b2 = {k: remote(pb2.at[piece((x + k) % 4, 128)], rb2.at[k - 1], x_peer(k)) for k in (2, 1, 3)}
+    step2 = ({}, {})
+    for j in (2, 1, 3, 0):
+        for n, (src, got, src2, got2, _, _, u, v, _, v_peer) in enumerate(parts):
+            mine = piece((v + j) % 4, 32)
+            value = src[piece(u * 4 + (v + j) % 4, 32), :].astype(F32)
+            for k in (1, 3, 2):
+                step1[n][j, k].wait_recv()
+                value = value + got[k - 1, mine, :].astype(F32)
+            src2[mine, :] = value.astype(BF16)
+            if j:
+                step2[n][j] = remote(src2.at[mine], got2.at[j - 1], v_peer(j))
 
     halves.wait_recv()
     sm0[...] = (sm[core] + sm_sib[...]).astype(BF16)
-    far = (4, 3, 5, 2, 6, 1, 7)
     s1 = {k: remote(sm0.at[piece((z + k) % 8, 48)], sz.at[k - 1], z_peer(k)) for k in far}
 
-    pa3[...] = add(pa2[piece(y, 128), :], ra2, a2)
-    a3 = {k: remote(pa3.at[piece((z + k) % 8, 16)], ra3.at[k - 1], z_peer(k)) for k in far}
-    pb3[...] = add(pb2[piece(x, 128), :], rb2, b2)
-    b3 = {k: remote(pb3.at[piece((z + k) % 8, 16)], rb3.at[k - 1], z_peer(k)) for k in far}
+    step3 = ({}, {})
+    for n, (_, _, src2, got2, src3, got3, _, v, _, _) in enumerate(parts):
+        src3[...] = add(src2[piece(v, 32), :], got2, step2[n])
+        for k in far:
+            step3[n][k] = remote(src3.at[cell((z + k) % 8)], got3.at[k - 1], z_peer(k))
 
     sx[x] = add(sm0[piece(z, 48), :], sz, s1)
-    s2 = [remote(sx.at[x], sx.at[x], x_peer(k)) for k in (2, 1, 3)]
-
-    a_own = x * 512 + y * 128
-    b_own = y * 512 + x * 128
-
-    def span(at, rows):
-        return pl.ds(pl.multiple_of(at, rows), rows)
-
-    big_ref[core, 0, span(a_own + z * 16, 16), :] = add(pa3[piece(z, 16), :], ra3, a3)
-    here = big_ref.at[core, 0, span(a_own + z * 16, 16)]
-    a4 = [remote(here, here, z_peer(k)) for k in far]
-    big_ref[core, 1, span(b_own + z * 16, 16), :] = add(pb3[piece(z, 16), :], rb3, b3)
-    here_b = big_ref.at[core, 1, span(b_own + z * 16, 16)]
-    b4 = [remote(here_b, here_b, z_peer(k)) for k in far]
+    s2 = [remote(sx.at[x], sx.at[x], x_peer(k)) for k in far4]
+
+    def place(c, n, u, v, rows):
+        return pl.ds(pl.multiple_of(c * 1024 + n * 512 + u * 128 + v * 32, 32), rows)
+
+    step4 = ([], [])
+    for n, (_, _, _, _, src3, got3, u, v, _, _) in enumerate(parts):
+        block = big.at[place(core, n, u, v, 32)]
+        block[cell(z)] = add(src3[cell(z)], got3, step3[n])
+        for k in far:
+            here = block.at[cell(z)]
+            step4[n].append(remote(here, here, z_peer(k)))
 
     def four(ref):
         value = ref[0].astype(F32)
@@ -413,63 +435,101 @@
     for copy in s2:
         copy.wait_recv()
     sy[y] = four(sx)
-    s3 = [remote(sy.at[y], sy.at[y], y_peer(k)) for k in (2, 1, 3)]
-
-    for copy in a4:
-        copy.wait_recv()
-    mid = big_ref.at[core, 0, span(a_own, 128)]
-    a5 = [remote(mid, mid, y_peer(k)) for k in (2, 1, 3)]
-    for copy in b4:
-        copy.wait_recv()
-    mid_b = big_ref.at[core, 1, span(b_own, 128)]
-    b5 = [remote(mid_b, mid_b, x_peer(k)) for k in (2, 1, 3)]
+    s3 = [remote(sy.at[y], sy.at[y], y_peer(k)) for k in far4]
+
+    step5 = ({}, {})
+    step6 = ({}, {})
+
+    def forward(n, m):
+        u, v, u_peer = parts[n][6], parts[n][7], parts[n][8]
+        block = big.at[place(core, n, u, (v + 4 - m) % 4, 32)]
+        for k in far4:
+            step6[n][m, k] = remote(block, block, u_peer(k))
+
+    for n in range(2):
+        u, v, v_peer = parts[n][6], parts[n][7], parts[n][9]
+        for copy in step4[n]:
+            copy.wait_recv()
+        block = big.at[place(core, n, u, v, 32)]
+        for k in far4:
+            step5[n][k] = remote(block, block, v_peer(k))
+        forward(n, 0)
 
     for copy in s3:
         copy.wait_recv()
-    small_ref[core, piece(z, 48), :] = four(sy)
-    bit = small_ref.at[core, piece(z, 48)]
+    small[core, piece(z, 48), :] = four(sy)
+    bit = small.at[core, piece(z, 48)]
     s4 = [remote(bit, bit, z_peer(k)) for k in far]
 
-    for copy in a5:
-        copy.wait_recv()
-    quarter = big_ref.at[core, 0, piece(x, 512)]
-    order = (2, 1, 3)
-    a6 = [remote(quarter, quarter, x_peer(k)) for k in order]
-    for copy in b5:
-        copy.wait_recv()
-    quarter_b = big_ref.at[core, 1, piece(y, 512)]
-    b6 = [remote(quarter_b, quarter_b, y_peer(k)) for k in order]
-
-    last = [remote(quarter, quarter, sibling), remote(quarter_b, quarter_b, sibling)]
+    for m in (1, 3, 2):
+        for n in range(2):
+            step5[n][m].wait_recv()
+            forward(n, m)
+
+    last = []
+
+    def cross(n, u):
+        chunk = place(core, n, u, 0, 128)
+        last.append((remote(big.at[chunk], big.at[chunk], sibling), place(other, n, u, 0, 128)))
+        keep(big.at[chunk], big_ref.at[chunk])
+
+    for n in range(2):
+        cross(n, parts[n][6])
     for copy in s4:
         copy.wait_recv()
-    last.append(remote(small_ref.at[core], small_ref.at[core], sibling))
-    for i in (1, 2, 0):
-        k = order[i]
-        a6[i].wait_recv()
-        got = big_ref.at[core, 0, piece((x + 4 - k) % 4, 512)]
-        last.append(remote(got, got, sibling))
-        b6[i].wait_recv()
-        got_b = big_ref.at[core, 1, piece((y + 4 - k) % 4, 512)]
-        last.append(remote(got_b, got_b, sibling))
-    for copy in last:
+    bits = remote(small.at[core], small.at[core], sibling)
+    keep(small.at[core], small_ref.at[core])
+    for k in (1, 3, 2):
+        for n in range(2):
+            for m in (0, 1, 3, 2):
+                step6[n][m, k].wait_recv()
+            cross(n, (parts[n][6] + 4 - k) % 4)
+    bits.wait_recv()
+    keep(small.at[other], small_ref.at[other])
+    for copy, chunk in last:
         copy.wait_recv()
+        keep(big.at[chunk], big_ref.at[chunk])
     for copy in started:
         copy.wait_send()
-
-
-N_SEM = 140
-
-
-def widen(big_ref, small_ref, in_ref, out_ref, mix_ref):
-    for j in range(4):
-        in_ref[:, j * 128 : (j + 1) * 128] = big_ref[0, j // 2, j % 2].astype(F32)
-
-    @pl.when((pl.program_id(0) == 0) & (pl.program_id(1) == 0))
-    def _():
-        for h in range(2):
-            out_ref[h * 256 : (h + 1) * 256, :] = small_ref[h, 0:256].astype(F32)
-            mix_ref[h * 128 : (h + 1) * 128, :] = small_ref[h, 256:384].astype(F32)
+    for copy in kept:
+        copy.wait()
+
+
+N_SEM = 160
+N_KEEP = 24
+
+
+STEPS = 8
+
+
+def widen(big_ref, small_ref, loss_ref, in_ref, out_ref, mix_ref, rows_ref, big, wide, small, small32, load_sem, store_sem):
+    size = FEATS // STEPS
+    loads = []
+    stores = [pltpu.make_async_copy(loss_ref, rows_ref, store_sem.at[STEPS])]
+    stores[0].start()
+    for i in range(STEPS):
+        rows = pl.ds(i * size, size)
+        loads.append(pltpu.make_async_copy(big_ref.at[rows], big.at[rows], load_sem.at[i]))
+    loads.append(pltpu.make_async_copy(small_ref, small, load_sem.at[STEPS]))
+    for load in loads:
+        load.start()
+    for i in range(STEPS):
+        rows = pl.ds(i * size, size)
+        loads[i].wait()
+        wide[rows, :] = big[rows, :].astype(F32)
+        stores.append(pltpu.make_async_copy(wide.at[rows], in_ref.at[rows], store_sem.at[i]))
+        stores[-1].start()
+    loads[STEPS].wait()
+    small32[...] = small[...].astype(F32)
+    for h in range(2):
+        at = small32.at[h, pl.ds(0, 256)]
+        stores.append(pltpu.make_async_copy(at, out_ref.at[pl.ds(h * 256, 256)], store_sem.at[STEPS + 1 + h]))
+        stores[-1].start()
+        at = small32.at[h, pl.ds(256, 128)]
+        stores.append(pltpu.make_async_copy(at, mix_ref.at[pl.ds(h * 128, 128)], store_sem.at[STEPS + 3 + h]))
+        stores[-1].start()
+    for store in stores:
+        store.wait()
 
 
 def on_device(patches, w_mix, w_in, w_out, partner_dev, partner_row):
@@ -493,28 +553,28 @@
         vmem((COUNT, FEATS), F32),
         vmem((2 * FREQS * COUNT, FILTERS), BF16),
         vmem((GROUP, EMBED), BF16),
-        vmem((PEERS * SLOT, COUNT), F32),
-        vmem((PEERS * SLOT, COUNT), F32),
-        vmem((PEERS * SLOT, EMBED), F32),
-        vmem((PEERS * SLOT, EMBED), F32),
-        vmem((PEERS * SLOT, EMBED), F32),
-        vmem((PEERS * SLOT, EMBED), F32),
-        vmem((CYCLE * SLOT, COUNT), F32),
+        vmem((PEERS, SLOT, COUNT), F32),
+        vmem((PEERS, SLOT, COUNT), F32),
+        vmem((PEERS, SLOT, COUNT), F32),
+        vmem((PEERS, SLOT, COUNT), F32),
+        vmem((PEERS, SLOT, COUNT), F32),
+        vmem((PEERS, SLOT, COUNT), F32),
+        vmem((CYCLE * TILE, COUNT), F32),
         vmem((FEATS // 2, COUNT), BF16),
         vmem((FEATS // 2, COUNT), BF16),
         vmem((FEATS // 2, COUNT), BF16),
         vmem((COUNT, HIDDEN), BF16),
         vmem((COUNT, HIDDEN), BF16),
-        vmem((2048, 128), BF16),
-        vmem((2048, 128), BF16),
-        vmem((3, 512, 128), BF16),
-        vmem((3, 512, 128), BF16),
-        vmem((512, 128), BF16),
-        vmem((512, 128), BF16),
-        vmem((3, 128, 128), BF16),
-        vmem((3, 128, 128), BF16),
-        vmem((128, 128), BF16),
-        vmem((128, 128), BF16),
+        vmem((512, 512), BF16),
+        vmem((512, 512), BF16),
+        vmem((3, 128, 512), BF16),
+        vmem((3, 128, 512), BF16),
+        vmem((128, 512), BF16),
+        vmem((128, 512), BF16),
+        vmem((3, 32, 512), BF16),
+        vmem((3, 32, 512), BF16),
+        vmem((32, 512), BF16),
+        vmem((32, 512), BF16),
         vmem((7, 16, 128), BF16),
         vmem((7, 16, 128), BF16),
         vmem((2, SMALL, 128), F32),
@@ -523,7 +583,11 @@
         vmem((7, 48, 128), BF16),
         vmem((4, 48, 128), BF16),
         vmem((4, 48, 128), BF16),
+        vmem((FEATS, HIDDEN), BF16),
+        vmem((2, SMALL, 128), BF16),
+        vmem((1, COUNT), F32),
         pltpu.SemaphoreType.DMA((12,)),
+        pltpu.SemaphoreType.DMA((N_KEEP,)),
         pltpu.SemaphoreType.DMA((N_SEM,)),
         pltpu.SemaphoreType.DMA((N_SEM,)),
     ]
@@ -532,11 +596,11 @@
         name="contrastive_step",
         out_shape=(
             jax.ShapeDtypeStruct((1, COUNT), F32),
-            jax.ShapeDtypeStruct((2, 2, 2048, 128), BF16),
+            jax.ShapeDtypeStruct((FEATS, HIDDEN), BF16),
             jax.ShapeDtypeStruct((2, SMALL, 128), BF16),
         ),
         in_specs=[vmem_spec, vmem_spec] + [any_spec] * 5,
-        out_specs=(vmem_spec, vmem_spec, vmem_spec),
+        out_specs=(any_spec, any_spec, any_spec),
         scratch_shapes=scratch,
         compiler_params=pltpu.CompilerParams(
             collective_id=0, has_side_effects=True, vmem_limit_bytes=56 * 2**20
@@ -550,27 +614,27 @@
         w_out,
         patches.reshape(COUNT * ANGLES, LANES),
     )
-    rows = 256
-    steps = FEATS // 2 // rows
-    g_in, g_out, g_mix = pl.pallas_call(
+    g_in, g_out, g_mix, loss = pl.pallas_call(
         widen,
         name="widen",
-        grid=(2, steps),
         out_shape=(
             jax.ShapeDtypeStruct((FEATS, HIDDEN), F32),
             jax.ShapeDtypeStruct((HIDDEN, EMBED), F32),
             jax.ShapeDtypeStruct((LANES, FILTERS), F32),
+            jax.ShapeDtypeStruct((1, COUNT), F32),
         ),
-        in_specs=[
-            pl.BlockSpec((1, 2, 2, rows, 128), lambda c, i: (c, 0, 0, i, 0)),
-            pl.BlockSpec((2, SMALL, 128), lambda c, i: (0, 0, 0)),
+        in_specs=[any_spec] * 3,
+        out_specs=(any_spec,) * 4,
+        scratch_shapes=[
+            vmem((FEATS, HIDDEN), BF16),
+            vmem((FEATS, HIDDEN), F32),
+            vmem((2, SMALL, 128), BF16),
+            vmem((2, SMALL, 128), F32),
+            pltpu.SemaphoreType.DMA((STEPS + 1,)),
+            pltpu.SemaphoreType.DMA((STEPS + 5,)),
         ],
-        out_specs=(
-            pl.BlockSpec((rows, HIDDEN), lambda c, i: (c * steps + i, 0)),
-            pl.BlockSpec((HIDDEN, EMBED), lambda c, i: (0, 0)),
-            pl.BlockSpec((LANES, FILTERS), lambda c, i: (0, 0)),
-        ),
-    )(big.reshape(2, 2, 2, FEATS // 2, 128), small)
+        compiler_params=pltpu.CompilerParams(vmem_limit_bytes=56 * 2**20),
+    )(big, small, loss)
     return (loss.reshape(COUNT), g_mix, g_in, g_out)
 
 

time: 79.9 us -> 71.3 us (0.89)
  Pallas kernels: 77.9 us -> 70.6 us
  local copies, waits for them, and re-layouts: 1.13 us -> 0 us
    pallas_call x1, Pallas kernels: 71.5 us -> 67.3 us  [on_device(): pl.pallas_call(kernel, name='contrastive_step', out_shape=(jax.ShapeDtype...]
    pallas_call x1, Pallas kernels: 6.36 us -> 3.29 us  [on_device(): pl.pallas_call(widen, name='widen', out_shape=(jax.ShapeDtypeStruct((FEAT...]
    unnamed x1 -> x0, local copies, waits for them, and re-layouts: 1.13 us -> none
where the time goes in v2:
time: 71.3 us; the launch traced here: 71.2 us
  Pallas kernels  70.6 us (99%)
    pallas_call x1, Pallas kernels, on_device(): pl.pallas_call(kernel, name='contrastive_step', out_shape=(jax.ShapeDtype...  67.3 us
    pallas_call x1, Pallas kernels, on_device(): pl.pallas_call(widen, name='widen', out_shape=(jax.ShapeDtypeStruct((FEAT...  3.29 us

profile of v2, /device:TPU:1, one launch (start us, length us, event | category | flops | bytes accessed | tf_op | source)
XLA Modules:
  0.0 71.2 jit_solution(8557809743881265202)
XLA Ops:
  0.6 67.3 %contrastive_step.1 = (f32[1,128]{1,0:T(1,128)}, bf16[2048,512]{1,0:T(8,128)(2,1)}, bf16[2,384,128]{2,1,0:T(8,128)(2,1)}) custom-call(s32[1,128]{1,0:T(1,128)} %bitcast.5, s32[1,128]{1,0:T(1,128)} %bitcast.6, bf16[256,512]{1,0:T(8,128)(2,1)} %constant.2.clone.table_hbm, bf16[256,128]{1,0:T(8,128)(2,1)} %wmix_hbm.1, bf16[2048,512]{1,0:T(8,128)(2,1)} %win_hbm.1, ...), custom_call_target="tpu_custom_call" | custom-call | tf_op jit(solution)/shard_map/contrastive_step/pallas_call | solution.py:594
  67.9 3.3 %widen.1 = (f32[2048,512]{1,0:T(8,128)}, f32[512,128]{1,0:T(8,128)}, f32[256,128]{1,0:T(8,128)}, f32[1,128]{1,0:T(1,128)}) custom-call(bf16[2048,512]{1,0:T(8,128)(2,1)} %get-tuple-element.11.big_ref, bf16[2,384,128]{2,1,0:T(8,128)(2,1)} %get-tuple-element.12.small_ref, f32[1,128]{1,0:T(1,128)} %get-tuple-element.13.loss_ref), custom_call_target="tpu_custom_call" | custom-call | tf_op jit(solution)/shard_map/widen/pallas_call | solution.py:617

commit v3 on v2

--- a/solution.py
+++ b/solution.py
@@ -63,9 +63,9 @@
 
 
 def kernel(
-    pdev_ref, prow_ref, table_hbm, wmix_hbm, win_hbm, wout_hbm, patches_hbm,
+    pdev_hbm, prow_hbm, table_hbm, wmix_hbm, win_hbm, wout_hbm, patches_hbm,
     loss_ref, big_ref, small_ref,
-    patches, table, wmix, win, wout,
+    pdev_ref, prow_ref, patches, table, wmix, win, wout,
     spec, spec_t, real, imag, feat, normed, preact, hid_t, ngrad, mixg,
     group, ask_out, ask_in, row_out, row_in, back_out, back_in, tot_all,
     nt_own, nt_send, nt_sib, gp_own, gp_sib,
@@ -76,24 +76,26 @@
 ):
     blk = lax.axis_index("blk")
     dp = lax.axis_index("dp")
-    y = blk // 2
-    x = (blk % 2) * 2 + dp // 16
-    z = (dp // 2) % 8
-    core = dp % 2
+    y = lax.div(blk, 2)
+    x_low = lax.div(dp, 16)
+    x = lax.rem(blk, 2) * 2 + x_low
+    z = lax.rem(lax.div(dp, 2), 8)
+    core = lax.rem(dp, 2)
     other = 1 - core
 
     def device(x_, y_, z_, c_):
-        return (y_ * 2 + x_ // 2, ((x_ % 2) * 8 + z_) * 2 + c_)
+        return (y_ * 2 + lax.div(x_, 2), lax.rem(x_, 2) * 16 + z_ * 2 + c_)
 
     sibling = device(x, y, z, other)
 
-    def dp_peer(i):
-        quad = i // 4
-        half = (quad + 1) // 2
-        dz = 4 + half * (2 * (quad % 2) - 1)
-        xl = (dp // 16 + 1 - (i % 4) // 2) % 2
-        c = (core + 1 - i % 2) % 2
-        return (xl * 8 + (z + dz) % 8) * 2 + c
+    dp_peers = []
+    for dz in (4, 5, 3, 6, 2, 7, 1, 0):
+        z_part = lax.rem(z + dz, 8) * 2
+        for x_part in ((1 - x_low) * 16, x_low * 16):
+            for c_part in (other, core):
+                dp_peers.append(x_part + z_part + c_part)
+    dp_peers = dp_peers[:-1]
+    blk_peers = [lax.rem(blk + step, CYCLE) for step in (5, 4, 3, 2, 1, 6, 7)]
 
     used = [0]
     started = []
@@ -115,21 +117,17 @@
         for p in range(PEERS):
             src[p] = value[p * SLOT : (p + 1) * SLOT]
 
-        def send(i, carry):
-            p = dp_peer(i)
+        for p in dp_peers:
             pltpu.make_async_remote_copy(
                 src_ref=src.at[p], dst_ref=dst.at[dp],
                 send_sem=send_sem.at[k], recv_sem=recv_sem.at[k],
                 device_id=(blk, p), device_id_type=MESH,
             ).start()
-            return carry
-
-        lax.fori_loop(0, PEERS - 1, send, 0)
         dst[dp] = src[dp]
         rows = pl.ds(0, PEERS - 1)
         whole = pltpu.make_async_remote_copy(
             src_ref=src.at[rows], dst_ref=dst.at[rows], send_sem=send_sem.at[k],
-            recv_sem=recv_sem.at[k], device_id=(blk, dp_peer(0)), device_id_type=MESH,
+            recv_sem=recv_sem.at[k], device_id=(blk, dp_peers[0]), device_id_type=MESH,
         )
         started.append(whole)
         return whole
@@ -141,16 +139,16 @@
         k = used[0]
         used[0] += 1
         mine = pl.ds(pl.multiple_of(blk * rows, rows), rows)
-        for step in (5, 4, 3, 2, 1, 6, 7):
+        for b in blk_peers:
             pltpu.make_async_remote_copy(
                 src_ref=ref.at[mine], dst_ref=ref.at[mine],
                 send_sem=send_sem.at[k], recv_sem=recv_sem.at[k],
-                device_id=((blk + step) % CYCLE, dp), device_id_type=MESH,
+                device_id=(b, dp), device_id_type=MESH,
             ).start()
         span = pl.ds(0, (CYCLE - 1) * rows)
         whole = pltpu.make_async_remote_copy(
             src_ref=ref.at[span], dst_ref=ref.at[span], send_sem=send_sem.at[k],
-            recv_sem=recv_sem.at[k], device_id=((blk + 1) % CYCLE, dp), device_id_type=MESH,
+            recv_sem=recv_sem.at[k], device_id=(blk_peers[0], dp), device_id_type=MESH,
         )
         started.append(whole)
         return whole
@@ -161,6 +159,14 @@
         copy = pltpu.make_async_copy(src, dst, keep_sem.at[len(kept)])
         copy.start()
         kept.append(copy)
+
+    barrier = pltpu.get_barrier_semaphore()
+
+    for p in dp_peers:
+        pl.semaphore_signal(barrier, inc=1, device_id=(blk, p), device_id_type=MESH)
+    for b in blk_peers:
+        pl.semaphore_signal(barrier, inc=1, device_id=(b, dp), device_id_type=MESH)
+    pl.semaphore_signal(barrier, inc=1, device_id=device(3 - x, y, z, core), device_id_type=MESH)
 
     chunk = 1024
     loads = [pltpu.make_async_copy(table_hbm, table, load_sem.at[0])]
@@ -170,20 +176,13 @@
     loads.append(pltpu.make_async_copy(wmix_hbm, wmix, load_sem.at[9]))
     loads.append(pltpu.make_async_copy(win_hbm, win, load_sem.at[10]))
     loads.append(pltpu.make_async_copy(wout_hbm, wout, load_sem.at[11]))
-    for load in loads:
-        load.start()
-
-    barrier = pltpu.get_barrier_semaphore()
-
-    def greet(i, carry):
-        pl.semaphore_signal(barrier, inc=1, device_id=(blk, dp_peer(i)), device_id_type=MESH)
-        return carry
-
-    lax.fori_loop(0, PEERS - 1, greet, 0)
-    for step in range(1, CYCLE):
-        pl.semaphore_signal(barrier, inc=1, device_id=((blk + step) % CYCLE, dp), device_id_type=MESH)
-    pl.semaphore_signal(barrier, inc=1, device_id=device(3 - x, y, z, core), device_id_type=MESH)
-
+    loads.append(pltpu.make_async_copy(pdev_hbm, pdev_ref, load_sem.at[12]))
+    loads.append(pltpu.make_async_copy(prow_hbm, prow_ref, load_sem.at[13]))
+    for i in (12, 13) + tuple(range(12)):
+        loads[i].start()
+
+    loads[12].wait()
+    loads[13].wait()
     lane = iota((COUNT, COUNT), 1)
     row = iota((COUNT, COUNT), 0)
     dev_lane = jnp.broadcast_to(pdev_ref[...], (COUNT, COUNT))
@@ -211,9 +210,9 @@
         for k in range(2 * FREQS):
             part = jnp.concatenate([low[k * 8 : k * 8 + 8], high[k * 8 : k * 8 + 8]], axis=0)
             spec[k * COUNT + g * 16 : k * COUNT + g * 16 + 16, :] = part.astype(BF16)
-
-    pl.semaphore_wait(barrier, PEERS - 1 + CYCLE - 1 + 1)
-    asked = spread(ask, ask_out, ask_in)
+        if g == 2:
+            pl.semaphore_wait(barrier, PEERS - 1 + CYCLE - 1 + 1)
+            asked = spread(ask, ask_out, ask_in)
 
     loads[9].wait()
     total = jnp.zeros((COUNT, 1), F32)
@@ -267,9 +266,6 @@
     for k in range(8):
         cols = pl.ds(pl.multiple_of(base + k * FILTERS, FILTERS), FILTERS)
         nt_own[k * FILTERS : (k + 1) * FILTERS, :] = normed[:, cols].T
-    hid_t[...] = hidden.T
-    for k in range(2 * FREQS):
-        spec_t[:, k * COUNT : (k + 1) * COUNT] = spec[k * COUNT : (k + 1) * COUNT, :].T
 
     gathered.wait_recv()
     keys = group[...]
@@ -295,6 +291,9 @@
     loss[...] = (jnp.log(tot_lane) - spos_lane)[:1]
     keep(loss, loss_ref)
     grad_units = away * positive + COEF * (numer / totals)
+    hid_t[...] = hidden.T
+    for k in range(2 * FREQS):
+        spec_t[:, k * COUNT : (k + 1) * COUNT] = spec[k * COUNT : (k + 1) * COUNT, :].T
 
     tots.wait_recv()
     inverse = jnp.concatenate(
@@ -329,24 +328,22 @@
         to = pa if i < 2 else pb
         to[(i % 2) * 256 : (i % 2 + 1) * 256, :] = prod.astype(BF16)
 
-    def x_peer(k):
-        return device((x + k) % 4, y, z, core)
-
-    def y_peer(k):
-        return device(x, (y + k) % 4, z, core)
-
-    def z_peer(k):
-        return device(x, y, (z + k) % 8, core)
+    xs = [lax.rem(x + k, 4) for k in range(4)]
+    ys = [lax.rem(y + k, 4) for k in range(4)]
+    zs = [lax.rem(z + k, 8) for k in range(8)]
+    x_peers = [device(xs[k], y, z, core) for k in range(4)]
+    y_peers = [device(x, ys[k], z, core) for k in range(4)]
+    z_peers = [device(x, y, zs[k], core) for k in range(8)]
 
     def piece(at, rows):
         return pl.ds(pl.multiple_of(at * rows, rows), rows)
 
     def cell(at):
-        return (piece(at // 4, 16), piece(at % 4, 128))
+        return (piece(lax.div(at, 4), 16), piece(lax.rem(at, 4), 128))
 
     parts = (
-        (pa, ra1, pa2, ra2, pa3, ra3, x, y, x_peer, y_peer),
-        (pb, rb1, pb2, rb2, pb3, rb3, y, x, y_peer, x_peer),
+        (pa, ra1, pa2, ra2, pa3, ra3, xs, ys, x_peers, y_peers),
+        (pb, rb1, pb2, rb2, pb3, rb3, ys, xs, y_peers, x_peers),
     )
     far4 = (2, 1, 3)
     far = (4, 3, 5, 2, 6, 1, 7)
@@ -355,9 +352,9 @@
         for n, (src, got, _, _, _, _, u, v, u_peer, _) in enumerate(parts):
             for k in far4:
                 step1[n][j, k] = remote(
-                    src.at[piece((u + k) % 4 * 4 + (v + j) % 4, 32)],
-                    got.at[k - 1, piece((v + j) % 4, 32)],
-                    u_peer(k),
+                    src.at[piece(u[k] * 4 + v[j], 32)],
+                    got.at[k - 1, piece(v[j], 32)],
+                    u_peer[k],
                 )
 
     acc = jnp.zeros((COUNT, FILTERS), F32)
@@ -393,38 +390,38 @@
     step2 = ({}, {})
     for j in (2, 1, 3, 0):
         for n, (src, got, src2, got2, _, _, u, v, _, v_peer) in enumerate(parts):
-            mine = piece((v + j) % 4, 32)
-            value = src[piece(u * 4 + (v + j) % 4, 32), :].astype(F32)
+            mine = piece(v[j], 32)
+            value = src[piece(u[0] * 4 + v[j], 32), :].astype(F32)
             for k in (1, 3, 2):
                 step1[n][j, k].wait_recv()
                 value = value + got[k - 1, mine, :].astype(F32)
             src2[mine, :] = value.astype(BF16)
             if j:
-                step2[n][j] = remote(src2.at[mine], got2.at[j - 1], v_peer(j))
+                step2[n][j] = remote(src2.at[mine], got2.at[j - 1], v_peer[j])
 
     halves.wait_recv()
     sm0[...] = (sm[core] + sm_sib[...]).astype(BF16)
-    s1 = {k: remote(sm0.at[piece((z + k) % 8, 48)], sz.at[k - 1], z_peer(k)) for k in far}
+    s1 = {k: remote(sm0.at[piece(zs[k], 48)], sz.at[k - 1], z_peers[k]) for k in far}
 
     step3 = ({}, {})
     for n, (_, _, src2, got2, src3, got3, _, v, _, _) in enumerate(parts):
-        src3[...] = add(src2[piece(v, 32), :], got2, step2[n])
+        src3[...] = add(src2[piece(v[0], 32), :], got2, step2[n])
         for k in far:
-            step3[n][k] = remote(src3.at[cell((z + k) % 8)], got3.at[k - 1], z_peer(k))
+            step3[n][k] = remote(src3.at[cell(zs[k])], got3.at[k - 1], z_peers[k])
 
     sx[x] = add(sm0[piece(z, 48), :], sz, s1)
-    s2 = [remote(sx.at[x], sx.at[x], x_peer(k)) for k in far4]
+    s2 = [remote(sx.at[x], sx.at[x], x_peers[k]) for k in far4]
 
     def place(c, n, u, v, rows):
         return pl.ds(pl.multiple_of(c * 1024 + n * 512 + u * 128 + v * 32, 32), rows)
 
     step4 = ([], [])
     for n, (_, _, _, _, src3, got3, u, v, _, _) in enumerate(parts):
-        block = big.at[place(core, n, u, v, 32)]
+        block = big.at[place(core, n, u[0], v[0], 32)]
         block[cell(z)] = add(src3[cell(z)], got3, step3[n])
         for k in far:
             here = block.at[cell(z)]
-            step4[n].append(remote(here, here, z_peer(k)))
+            step4[n].append(remote(here, here, z_peers[k]))
 
     def four(ref):
         value = ref[0].astype(F32)
@@ -435,31 +432,32 @@
     for copy in s2:
         copy.wait_recv()
     sy[y] = four(sx)
-    s3 = [remote(sy.at[y], sy.at[y], y_peer(k)) for k in far4]
+    s3 = [remote(sy.at[y], sy.at[y], y_peers[k]) for k in far4]
 
     step5 = ({}, {})
     step6 = ({}, {})
 
     def forward(n, m):
         u, v, u_peer = parts[n][6], parts[n][7], parts[n][8]
-        block = big.at[place(core, n, u, (v + 4 - m) % 4, 32)]
+        block = big.at[place(core, n, u[0], v[(4 - m) % 4], 32)]
         for k in far4:
-            step6[n][m, k] = remote(block, block, u_peer(k))
+            step6[n][m, k] = remote(block, block, u_peer[k])
 
     for n in range(2):
         u, v, v_peer = parts[n][6], parts[n][7], parts[n][9]
         for copy in step4[n]:
             copy.wait_recv()
-        block = big.at[place(core, n, u, v, 32)]
+        block = big.at[place(core, n, u[0], v[0], 32)]
         for k in far4:
-            step5[n][k] = remote(block, block, v_peer(k))
+            step5[n][k] = remote(block, block, v_peer[k])
+    for n in range(2):
         forward(n, 0)
 
     for copy in s3:
         copy.wait_recv()
     small[core, piece(z, 48), :] = four(sy)
     bit = small.at[core, piece(z, 48)]
-    s4 = [remote(bit, bit, z_peer(k)) for k in far]
+    s4 = [remote(bit, bit, z_peers[k]) for k in far]
 
     for m in (1, 3, 2):
         for n in range(2):
@@ -474,7 +472,7 @@
         keep(big.at[chunk], big_ref.at[chunk])
 
     for n in range(2):
-        cross(n, parts[n][6])
+        cross(n, parts[n][6][0])
     for copy in s4:
         copy.wait_recv()
     bits = remote(small.at[core], small.at[core], sibling)
@@ -483,7 +481,7 @@
         for n in range(2):
             for m in (0, 1, 3, 2):
                 step6[n][m, k].wait_recv()
-            cross(n, (parts[n][6] + 4 - k) % 4)
+            cross(n, parts[n][6][4 - k])
     bits.wait_recv()
     keep(small.at[other], small_ref.at[other])
     for copy, chunk in last:
@@ -535,8 +533,9 @@
 def on_device(patches, w_mix, w_in, w_out, partner_dev, partner_row):
     vmem = pltpu.VMEM
     any_spec = pl.BlockSpec(memory_space=pl.ANY)
-    vmem_spec = pl.BlockSpec(memory_space=pltpu.VMEM)
     scratch = [
+        vmem((1, COUNT), jnp.int32),
+        vmem((1, COUNT), jnp.int32),
         vmem((COUNT * ANGLES, LANES), BF16),
         vmem((256, 512), BF16),
         vmem((LANES, FILTERS), BF16),
@@ -586,7 +585,7 @@
         vmem((FEATS, HIDDEN), BF16),
         vmem((2, SMALL, 128), BF16),
         vmem((1, COUNT), F32),
-        pltpu.SemaphoreType.DMA((12,)),
+        pltpu.SemaphoreType.DMA((14,)),
         pltpu.SemaphoreType.DMA((N_KEEP,)),
         pltpu.SemaphoreType.DMA((N_SEM,)),
         pltpu.SemaphoreType.DMA((N_SEM,)),
@@ -599,7 +598,7 @@
             jax.ShapeDtypeStruct((FEATS, HIDDEN), BF16),
             jax.ShapeDtypeStruct((2, SMALL, 128), BF16),
         ),
-        in_specs=[vmem_spec, vmem_spec] + [any_spec] * 5,
+        in_specs=[any_spec] * 7,
         out_specs=(any_spec, any_spec, any_spec),
         scratch_shapes=scratch,
         compiler_params=pltpu.CompilerParams(

time: 71.3 us -> 68.8 us (0.965)
  Pallas kernels: 70.6 us -> 68 us
    pallas_call x1, Pallas kernels: 67.3 us -> 64.7 us  [on_device(): pl.pallas_call(kernel, name='contrastive_step', out_shape=(jax.ShapeDtype...]
where the time goes in v3:
time: 68.8 us; the launch traced here: 68.7 us
  Pallas kernels  68 us (99%)
    pallas_call x1, Pallas kernels, on_device(): pl.pallas_call(kernel, name='contrastive_step', out_shape=(jax.ShapeDtype...  64.7 us
    pallas_call x1, Pallas kernels, on_device(): pl.pallas_call(widen, name='widen', out_shape=(jax.ShapeDtypeStruct((FEAT...  3.29 us

profile of v3, /device:TPU:1, one launch (start us, length us, event | category | flops | bytes accessed | tf_op | source)
XLA Modules:
  0.0 68.7 jit_solution(11645568463030796437)
XLA Ops:
  0.6 64.7 %contrastive_step.1 = (f32[1,128]{1,0:T(1,128)}, bf16[2048,512]{1,0:T(8,128)(2,1)}, bf16[2,384,128]{2,1,0:T(8,128)(2,1)}) custom-call(s32[1,128]{1,0:T(1,128)} %bitcast.5, s32[1,128]{1,0:T(1,128)} %bitcast.6, bf16[256,512]{1,0:T(8,128)(2,1)} %constant.2.clone.table_hbm, bf16[256,128]{1,0:T(8,128)(2,1)} %wmix_hbm.1, bf16[2048,512]{1,0:T(8,128)(2,1)} %win_hbm.1, ...), custom_call_target="tpu_custom_call" | custom-call | tf_op jit(solution)/shard_map/contrastive_step/pallas_call | solution.py:593
  65.4 3.3 %widen.1 = (f32[2048,512]{1,0:T(8,128)}, f32[512,128]{1,0:T(8,128)}, f32[256,128]{1,0:T(8,128)}, f32[1,128]{1,0:T(1,128)}) custom-call(bf16[2048,512]{1,0:T(8,128)(2,1)} %get-tuple-element.11.big_ref, bf16[2,384,128]{2,1,0:T(8,128)(2,1)} %get-tuple-element.12.small_ref, f32[1,128]{1,0:T(1,128)} %get-tuple-element.13.loss_ref), custom_call_target="tpu_custom_call" | custom-call | tf_op jit(solution)/shard_map/widen/pallas_call | solution.py:616

commit v4 on v3

--- a/solution.py
+++ b/solution.py
@@ -39,10 +39,10 @@
         2.0 * math.pi / ANGLES
     )
     table = np.concatenate([np.cos(phase), -np.sin(phase)], axis=1)
-    wide = np.zeros((2 * FREQS, 8, 8, ANGLES), np.float32)
-    for n in range(8):
+    wide = np.zeros((2 * FREQS, 4, 4, ANGLES), np.float32)
+    for n in range(4):
         wide[:, n, n, :] = table.T
-    return wide.reshape(2 * FREQS * 8, 8 * ANGLES).astype(ml_dtypes.bfloat16)
+    return wide.reshape(2 * FREQS * 4, 4 * ANGLES).astype(ml_dtypes.bfloat16)
 
 
 def dot(a, b):
@@ -69,7 +69,7 @@
     spec, spec_t, real, imag, feat, normed, preact, hid_t, ngrad, mixg,
     group, ask_out, ask_in, row_out, row_in, back_out, back_in, tot_all,
     nt_own, nt_send, nt_sib, gp_own, gp_sib,
-    pa, pb, ra1, rb1, pa2, pb2, ra2, rb2, pa3, pb3, ra3, rb3,
+    pa, pb, ra1, rb1, pa2, pb2, ra2, rb2, cells, cells_in, done,
     sm, sm_sib, sm0, sz, sx, sy,
     big, small, loss,
     load_sem, keep_sem, send_sem, recv_sem,
@@ -205,10 +205,9 @@
     bank = table[...]
     for g in range(8):
         loads[1 + g].wait()
-        low = dot(bank, patches[g * chunk : g * chunk + 512, :])
-        high = dot(bank, patches[g * chunk + 512 : (g + 1) * chunk, :])
+        quads = [dot(bank, patches[g * chunk + q * 256 : g * chunk + (q + 1) * 256, :]) for q in range(4)]
         for k in range(2 * FREQS):
-            part = jnp.concatenate([low[k * 8 : k * 8 + 8], high[k * 8 : k * 8 + 8]], axis=0)
+            part = jnp.concatenate([quad[k * 4 : k * 4 + 4] for quad in quads], axis=0)
             spec[k * COUNT + g * 16 : k * COUNT + g * 16 + 16, :] = part.astype(BF16)
         if g == 2:
             pl.semaphore_wait(barrier, PEERS - 1 + CYCLE - 1 + 1)
@@ -322,11 +321,11 @@
     factor.wait_recv()
     sent.wait_recv()
     right = jnp.concatenate([gp_own[...], gp_sib[...]], axis=0)
-    for i in range(4):
-        rows = slice(i * 256, (i + 1) * 256)
-        prod = dot(jnp.concatenate([nt_own[rows, :], nt_sib[rows, :]], axis=1), right)
-        to = pa if i < 2 else pb
-        to[(i % 2) * 256 : (i % 2 + 1) * 256, :] = prod.astype(BF16)
+    def multiply(to, n):
+        for i in range(2):
+            rows = slice(n * 512 + i * 256, n * 512 + (i + 1) * 256)
+            prod = dot(jnp.concatenate([nt_own[rows, :], nt_sib[rows, :]], axis=1), right)
+            to[i * 256 : (i + 1) * 256, :] = prod.astype(BF16)
 
     xs = [lax.rem(x + k, 4) for k in range(4)]
     ys = [lax.rem(y + k, 4) for k in range(4)]
@@ -338,18 +337,16 @@
     def piece(at, rows):
         return pl.ds(pl.multiple_of(at * rows, rows), rows)
 
-    def cell(at):
-        return (piece(lax.div(at, 4), 16), piece(lax.rem(at, 4), 128))
-
     parts = (
-        (pa, ra1, pa2, ra2, pa3, ra3, xs, ys, x_peers, y_peers),
-        (pb, rb1, pb2, rb2, pb3, rb3, ys, xs, y_peers, x_peers),
+        (pa, ra1, pa2, ra2, xs, ys, x_peers, y_peers),
+        (pb, rb1, pb2, rb2, ys, xs, y_peers, x_peers),
     )
     far4 = (2, 1, 3)
     far = (4, 3, 5, 2, 6, 1, 7)
     step1 = ({}, {})
-    for j in (2, 1, 3, 0):
-        for n, (src, got, _, _, _, _, u, v, u_peer, _) in enumerate(parts):
+    for n, (src, got, _, _, u, v, u_peer, _) in enumerate(parts):
+        multiply(src, n)
+        for j in (2, 1, 3, 0):
             for k in far4:
                 step1[n][j, k] = remote(
                     src.at[piece(u[k] * 4 + v[j], 32)],
@@ -389,7 +386,7 @@
 
     step2 = ({}, {})
     for j in (2, 1, 3, 0):
-        for n, (src, got, src2, got2, _, _, u, v, _, v_peer) in enumerate(parts):
+        for n, (src, got, src2, got2, u, v, _, v_peer) in enumerate(parts):
             mine = piece(v[j], 32)
             value = src[piece(u[0] * 4 + v[j], 32), :].astype(F32)
             for k in (1, 3, 2):
@@ -403,11 +400,13 @@
     sm0[...] = (sm[core] + sm_sib[...]).astype(BF16)
     s1 = {k: remote(sm0.at[piece(zs[k], 48)], sz.at[k - 1], z_peers[k]) for k in far}
 
-    step3 = ({}, {})
-    for n, (_, _, src2, got2, src3, got3, _, v, _, _) in enumerate(parts):
-        src3[...] = add(src2[piece(v[0], 32), :], got2, step2[n])
-        for k in far:
-            step3[n][k] = remote(src3.at[cell(zs[k])], got3.at[k - 1], z_peers[k])
+    for n, (_, _, src2, got2, _, v, _, _) in enumerate(parts):
+        value = add(src2[piece(v[0], 32), :], got2, step2[n])
+        for at in range(8):
+            cells[at, n * 16 : n * 16 + 16, :] = value[
+                at // 4 * 16 : at // 4 * 16 + 16, at % 4 * 128 : at % 4 * 128 + 128
+            ]
+    step3 = {k: remote(cells.at[zs[k]], cells_in.at[k - 1], z_peers[k]) for k in far}
 
     sx[x] = add(sm0[piece(z, 48), :], sz, s1)
     s2 = [remote(sx.at[x], sx.at[x], x_peers[k]) for k in far4]
@@ -415,13 +414,8 @@
     def place(c, n, u, v, rows):
         return pl.ds(pl.multiple_of(c * 1024 + n * 512 + u * 128 + v * 32, 32), rows)
 
-    step4 = ([], [])
-    for n, (_, _, _, _, src3, got3, u, v, _, _) in enumerate(parts):
-        block = big.at[place(core, n, u[0], v[0], 32)]
-        block[cell(z)] = add(src3[cell(z)], got3, step3[n])
-        for k in far:
-            here = block.at[cell(z)]
-            step4[n].append(remote(here, here, z_peers[k]))
+    done[z] = add(cells[z], cells_in, step3)
+    step4 = [remote(done.at[z], done.at[z], z_peers[k]) for k in far]
 
     def four(ref):
         value = ref[0].astype(F32)
@@ -438,15 +432,18 @@
     step6 = ({}, {})
 
     def forward(n, m):
-        u, v, u_peer = parts[n][6], parts[n][7], parts[n][8]
+        u, v, u_peer = parts[n][4], parts[n][5], parts[n][6]
         block = big.at[place(core, n, u[0], v[(4 - m) % 4], 32)]
         for k in far4:
             step6[n][m, k] = remote(block, block, u_peer[k])
 
+    for copy in step4:
+        copy.wait_recv()
     for n in range(2):
-        u, v, v_peer = parts[n][6], parts[n][7], parts[n][9]
-        for copy in step4[n]:
-            copy.wait_recv()
+        u, v, v_peer = parts[n][4], parts[n][5], parts[n][7]
+        for at in range(8):
+            rows = pl.ds(pl.multiple_of(core * 1024 + n * 512 + u[0] * 128 + v[0] * 32 + at // 4 * 16, 16), 16)
+            big[rows, at % 4 * 128 : at % 4 * 128 + 128] = done[at, n * 16 : n * 16 + 16, :]
         block = big.at[place(core, n, u[0], v[0], 32)]
         for k in far4:
             step5[n][k] = remote(block, block, v_peer[k])
@@ -468,25 +465,22 @@
 
     def cross(n, u):
         chunk = place(core, n, u, 0, 128)
-        last.append((remote(big.at[chunk], big.at[chunk], sibling), place(other, n, u, 0, 128)))
+        last.append(remote(big.at[chunk], big_ref.at[chunk], sibling))
         keep(big.at[chunk], big_ref.at[chunk])
 
     for n in range(2):
-        cross(n, parts[n][6][0])
+        cross(n, parts[n][4][0])
     for copy in s4:
         copy.wait_recv()
-    bits = remote(small.at[core], small.at[core], sibling)
+    last.append(remote(small.at[core], small_ref.at[core], sibling))
     keep(small.at[core], small_ref.at[core])
     for k in (1, 3, 2):
         for n in range(2):
             for m in (0, 1, 3, 2):
                 step6[n][m, k].wait_recv()
-            cross(n, parts[n][6][4 - k])
-    bits.wait_recv()
-    keep(small.at[other], small_ref.at[other])
-    for copy, chunk in last:
+            cross(n, parts[n][4][4 - k])
+    for copy in last:
         copy.wait_recv()
-        keep(big.at[chunk], big_ref.at[chunk])
     for copy in started:
         copy.wait_send()
     for copy in kept:
@@ -537,7 +531,7 @@
         vmem((1, COUNT), jnp.int32),
         vmem((1, COUNT), jnp.int32),
         vmem((COUNT * ANGLES, LANES), BF16),
-        vmem((256, 512), BF16),
+        vmem((128, 256), BF16),
         vmem((LANES, FILTERS), BF16),
         vmem((FEATS, HIDDEN), BF16),
         vmem((HIDDEN, EMBED), BF16),
@@ -572,10 +566,9 @@
         vmem((128, 512), BF16),
         vmem((3, 32, 512), BF16),
         vmem((3, 32, 512), BF16),
-        vmem((32, 512), BF16),
-        vmem((32, 512), BF16),
-        vmem((7, 16, 128), BF16),
-        vmem((7, 16, 128), BF16),
+        vmem((8, 32, 128), BF16),
+        vmem((7, 32, 128), BF16),
+        vmem((8, 32, 128), BF16),
         vmem((2, SMALL, 128), F32),
         vmem((SMALL, 128), F32),
         vmem((SMALL, 128), BF16),

time: 68.8 us -> 68.9 us (level)
  no operation moved by 1% of the time
where the time goes in v4:
time: 68.9 us; the launch traced here: 68.7 us
  Pallas kernels  68.1 us (99%)
    pallas_call x1, Pallas kernels, on_device(): pl.pallas_call(kernel, name='contrastive_step', out_shape=(jax.ShapeDtype...  64.8 us
    pallas_call x1, Pallas kernels, on_device(): pl.pallas_call(widen, name='widen', out_shape=(jax.ShapeDtypeStruct((FEAT...  3.29 us

profile of v4, /device:TPU:1, one launch (start us, length us, event | category | flops | bytes accessed | tf_op | source)
XLA Modules:
  0.0 68.7 jit_solution(6533476435199999090)
XLA Ops:
  0.6 64.8 %contrastive_step.1 = (f32[1,128]{1,0:T(1,128)}, bf16[2048,512]{1,0:T(8,128)(2,1)}, bf16[2,384,128]{2,1,0:T(8,128)(2,1)}) custom-call(s32[1,128]{1,0:T(1,128)} %bitcast.5, s32[1,128]{1,0:T(1,128)} %bitcast.6, bf16[128,256]{1,0:T(8,128)(2,1)} %constant.2.clone.table_hbm, bf16[256,128]{1,0:T(8,128)(2,1)} %wmix_hbm.1, bf16[2048,512]{1,0:T(8,128)(2,1)} %win_hbm.1, ...), custom_call_target="tpu_custom_call" | custom-call | tf_op jit(solution)/shard_map/contrastive_step/pallas_call | solution.py:586
  65.5 3.3 %widen.1 = (f32[2048,512]{1,0:T(8,128)}, f32[512,128]{1,0:T(8,128)}, f32[256,128]{1,0:T(8,128)}, f32[1,128]{1,0:T(1,128)}) custom-call(bf16[2048,512]{1,0:T(8,128)(2,1)} %get-tuple-element.11.big_ref, bf16[2,384,128]{2,1,0:T(8,128)(2,1)} %get-tuple-element.12.small_ref, f32[1,128]{1,0:T(1,128)} %get-tuple-element.13.loss_ref), custom_call_target="tpu_custom_call" | custom-call | tf_op jit(solution)/shard_map/widen/pallas_call | solution.py:609

commit v5 on v4

--- a/solution.py
+++ b/solution.py
@@ -99,6 +99,13 @@
 
     used = [0]
     started = []
+
+    settled = [0]
+
+    def settle(upto):
+        for copy in started[settled[0] : upto]:
+            copy.wait_send()
+        settled[0] = max(settled[0], upto)
 
     def remote(src, dst, to):
         k = used[0]
@@ -400,6 +407,7 @@
     sm0[...] = (sm[core] + sm_sib[...]).astype(BF16)
     s1 = {k: remote(sm0.at[piece(zs[k], 48)], sz.at[k - 1], z_peers[k]) for k in far}
 
+    before_z = len(started)
     for n, (_, _, src2, got2, _, v, _, _) in enumerate(parts):
         value = add(src2[piece(v[0], 32), :], got2, step2[n])
         for at in range(8):
@@ -423,11 +431,13 @@
             value = value + ref[i].astype(F32)
         return value.astype(BF16)
 
+    settle(before_z)
     for copy in s2:
         copy.wait_recv()
     sy[y] = four(sx)
     s3 = [remote(sy.at[y], sy.at[y], y_peers[k]) for k in far4]
 
+    before_gather = len(started) - 3
     step5 = ({}, {})
     step6 = ({}, {})
 
@@ -470,19 +480,22 @@
 
     for n in range(2):
         cross(n, parts[n][4][0])
+    settle(before_gather)
     for copy in s4:
         copy.wait_recv()
     last.append(remote(small.at[core], small_ref.at[core], sibling))
     keep(small.at[core], small_ref.at[core])
+    before_last = len(started)
     for k in (1, 3, 2):
+        if k == 2:
+            settle(before_last)
         for n in range(2):
             for m in (0, 1, 3, 2):
                 step6[n][m, k].wait_recv()
             cross(n, parts[n][4][4 - k])
     for copy in last:
         copy.wait_recv()
-    for copy in started:
-        copy.wait_send()
+    settle(len(started))
     for copy in kept:
         copy.wait()
 

time: 68.9 us -> 68.7 us (level)
  no operation moved by 1% of the time
where the time goes in v5:
time: 68.7 us; the launch traced here: 68.6 us
  Pallas kernels  67.9 us (99%)
    pallas_call x1, Pallas kernels, on_device(): pl.pallas_call(kernel, name='contrastive_step', out_shape=(jax.ShapeDtype...  64.6 us
    pallas_call x1, Pallas kernels, on_device(): pl.pallas_call(widen, name='widen', out_shape=(jax.ShapeDtypeStruct((FEAT...  3.29 us

profile of v5, /device:TPU:1, one launch (start us, length us, event | category | flops | bytes accessed | tf_op | source)
XLA Modules:
  0.0 68.6 jit_solution(3218537419239357031)
XLA Ops:
  0.6 64.6 %contrastive_step.1 = (f32[1,128]{1,0:T(1,128)}, bf16[2048,512]{1,0:T(8,128)(2,1)}, bf16[2,384,128]{2,1,0:T(8,128)(2,1)}) custom-call(s32[1,128]{1,0:T(1,128)} %bitcast.5, s32[1,128]{1,0:T(1,128)} %bitcast.6, bf16[128,256]{1,0:T(8,128)(2,1)} %constant.2.clone.table_hbm, bf16[256,128]{1,0:T(8,128)(2,1)} %wmix_hbm.1, bf16[2048,512]{1,0:T(8,128)(2,1)} %win_hbm.1, ...), custom_call_target="tpu_custom_call" | custom-call | tf_op jit(solution)/shard_map/contrastive_step/pallas_call | solution.py:599
  65.3 3.3 %widen.1 = (f32[2048,512]{1,0:T(8,128)}, f32[512,128]{1,0:T(8,128)}, f32[256,128]{1,0:T(8,128)}, f32[1,128]{1,0:T(1,128)}) custom-call(bf16[2048,512]{1,0:T(8,128)(2,1)} %get-tuple-element.11.big_ref, bf16[2,384,128]{2,1,0:T(8,128)(2,1)} %get-tuple-element.12.small_ref, f32[1,128]{1,0:T(1,128)} %get-tuple-element.13.loss_ref), custom_call_target="tpu_custom_call" | custom-call | tf_op jit(solution)/shard_map/widen/pallas_call | solution.py:622

commit v6 on v3

--- a/solution.py
+++ b/solution.py
@@ -39,10 +39,10 @@
         2.0 * math.pi / ANGLES
     )
     table = np.concatenate([np.cos(phase), -np.sin(phase)], axis=1)
-    wide = np.zeros((2 * FREQS, 8, 8, ANGLES), np.float32)
-    for n in range(8):
+    wide = np.zeros((2 * FREQS, 4, 4, ANGLES), np.float32)
+    for n in range(4):
         wide[:, n, n, :] = table.T
-    return wide.reshape(2 * FREQS * 8, 8 * ANGLES).astype(ml_dtypes.bfloat16)
+    return wide.reshape(2 * FREQS * 4, 4 * ANGLES).astype(ml_dtypes.bfloat16)
 
 
 def dot(a, b):
@@ -205,10 +205,9 @@
     bank = table[...]
     for g in range(8):
         loads[1 + g].wait()
-        low = dot(bank, patches[g * chunk : g * chunk + 512, :])
-        high = dot(bank, patches[g * chunk + 512 : (g + 1) * chunk, :])
+        quads = [dot(bank, patches[g * chunk + q * 256 : g * chunk + (q + 1) * 256, :]) for q in range(4)]
         for k in range(2 * FREQS):
-            part = jnp.concatenate([low[k * 8 : k * 8 + 8], high[k * 8 : k * 8 + 8]], axis=0)
+            part = jnp.concatenate([quad[k * 4 : k * 4 + 4] for quad in quads], axis=0)
             spec[k * COUNT + g * 16 : k * COUNT + g * 16 + 16, :] = part.astype(BF16)
         if g == 2:
             pl.semaphore_wait(barrier, PEERS - 1 + CYCLE - 1 + 1)
@@ -322,11 +321,11 @@
     factor.wait_recv()
     sent.wait_recv()
     right = jnp.concatenate([gp_own[...], gp_sib[...]], axis=0)
-    for i in range(4):
-        rows = slice(i * 256, (i + 1) * 256)
-        prod = dot(jnp.concatenate([nt_own[rows, :], nt_sib[rows, :]], axis=1), right)
-        to = pa if i < 2 else pb
-        to[(i % 2) * 256 : (i % 2 + 1) * 256, :] = prod.astype(BF16)
+    def multiply(to, n):
+        for i in range(2):
+            rows = slice(n * 512 + i * 256, n * 512 + (i + 1) * 256)
+            prod = dot(jnp.concatenate([nt_own[rows, :], nt_sib[rows, :]], axis=1), right)
+            to[i * 256 : (i + 1) * 256, :] = prod.astype(BF16)
 
     xs = [lax.rem(x + k, 4) for k in range(4)]
     ys = [lax.rem(y + k, 4) for k in range(4)]
@@ -348,8 +347,9 @@
     far4 = (2, 1, 3)
     far = (4, 3, 5, 2, 6, 1, 7)
     step1 = ({}, {})
-    for j in (2, 1, 3, 0):
-        for n, (src, got, _, _, _, _, u, v, u_peer, _) in enumerate(parts):
+    for n, (src, got, _, _, _, _, u, v, u_peer, _) in enumerate(parts):
+        multiply(src, n)
+        for j in (2, 1, 3, 0):
             for k in far4:
                 step1[n][j, k] = remote(
                     src.at[piece(u[k] * 4 + v[j], 32)],
@@ -468,25 +468,22 @@
 
     def cross(n, u):
         chunk = place(core, n, u, 0, 128)
-        last.append((remote(big.at[chunk], big.at[chunk], sibling), place(other, n, u, 0, 128)))
+        last.append(remote(big.at[chunk], big_ref.at[chunk], sibling))
         keep(big.at[chunk], big_ref.at[chunk])
 
     for n in range(2):
         cross(n, parts[n][6][0])
     for copy in s4:
         copy.wait_recv()
-    bits = remote(small.at[core], small.at[core], sibling)
+    last.append(remote(small.at[core], small_ref.at[core], sibling))
     keep(small.at[core], small_ref.at[core])
     for k in (1, 3, 2):
         for n in range(2):
             for m in (0, 1, 3, 2):
                 step6[n][m, k].wait_recv()
             cross(n, parts[n][6][4 - k])
-    bits.wait_recv()
-    keep(small.at[other], small_ref.at[other])
-    for copy, chunk in last:
+    for copy in last:
         copy.wait_recv()
-        keep(big.at[chunk], big_ref.at[chunk])
     for copy in started:
         copy.wait_send()
     for copy in kept:
@@ -537,7 +534,7 @@
         vmem((1, COUNT), jnp.int32),
         vmem((1, COUNT), jnp.int32),
         vmem((COUNT * ANGLES, LANES), BF16),
-        vmem((256, 512), BF16),
+        vmem((128, 256), BF16),
         vmem((LANES, FILTERS), BF16),
         vmem((FEATS, HIDDEN), BF16),
         vmem((HIDDEN, EMBED), BF16),

time: 68.8 us -> 68.5 us (level)
  no operation moved by 1% of the time
where the time goes in v6:
time: 68.5 us; the launch traced here: 68.4 us
  Pallas kernels  67.8 us (99%)
    pallas_call x1, Pallas kernels, on_device(): pl.pallas_call(kernel, name='contrastive_step', out_shape=(jax.ShapeDtype...  64.5 us
    pallas_call x1, Pallas kernels, on_device(): pl.pallas_call(widen, name='widen', out_shape=(jax.ShapeDtypeStruct((FEAT...  3.29 us

profile of v6, /device:TPU:1, one launch (start us, length us, event | category | flops | bytes accessed | tf_op | source)
XLA Modules:
  0.0 68.4 jit_solution(13005971728470552472)
XLA Ops:
  0.6 64.5 %contrastive_step.1 = (f32[1,128]{1,0:T(1,128)}, bf16[2048,512]{1,0:T(8,128)(2,1)}, bf16[2,384,128]{2,1,0:T(8,128)(2,1)}) custom-call(s32[1,128]{1,0:T(1,128)} %bitcast.5, s32[1,128]{1,0:T(1,128)} %bitcast.6, bf16[128,256]{1,0:T(8,128)(2,1)} %constant.2.clone.table_hbm, bf16[256,128]{1,0:T(8,128)(2,1)} %wmix_hbm.1, bf16[2048,512]{1,0:T(8,128)(2,1)} %win_hbm.1, ...), custom_call_target="tpu_custom_call" | custom-call | tf_op jit(solution)/shard_map/contrastive_step/pallas_call | solution.py:590
  65.1 3.3 %widen.1 = (f32[2048,512]{1,0:T(8,128)}, f32[512,128]{1,0:T(8,128)}, f32[256,128]{1,0:T(8,128)}, f32[1,128]{1,0:T(1,128)}) custom-call(bf16[2048,512]{1,0:T(8,128)(2,1)} %get-tuple-element.11.big_ref, bf16[2,384,128]{2,1,0:T(8,128)(2,1)} %get-tuple-element.12.small_ref, f32[1,128]{1,0:T(1,128)} %get-tuple-element.13.loss_ref), custom_call_target="tpu_custom_call" | custom-call | tf_op jit(solution)/shard_map/widen/pallas_call | solution.py:613
